TPU v7x, 32 devices: a whole 2x2x4 slice. The times are simulated.
32 devices in a mesh: gz: 4 (over y, core), xy: 8 (over z, x).
Axes of the slice: x: 2, y: 2, z: 4, core: 2. Of those that a mesh axis runs over, the one named last changes fastest.
Arguments:
- density: float32 [128, 256, 1024], P('gz', 'xy')
- uptake: float32 [128, 256, 1024], P('gz', 'xy'), may hold values from 0.5 to 50
- brick_values: bfloat16 [2304, 4096], P(('gz', 'xy'))
- brick_ids: int32 [2304], P(('gz', 'xy')), may hold values from 0 to 8191, as said below
- slot_counts: int32 [32, 9], P(('gz', 'xy')), may hold values from 0 to 8, as said below
Outputs:
- supply: float32 [128, 256, 1024], P('gz', 'xy')
- concentration: float32 [128, 256, 1024], P('gz', 'xy')
Inputs may be any that keep to these rules, and one draw needn't show every extreme that they name: `brick_ids`: the slots 8 j to 8 j + 7 of each device (j = 0 to 8) name bricks of the device whose gz index differs by j // 3 - 1 and whose xy index differs by j % 3 - 1, or of the device itself where no such device exists; the first and the last brick of the grid are both named. `slot_counts`: entry j of a device counts the live slots at the start of its block j; it is 0 where block j's device does not exist, and 8 for j = 4.
All inputs are finite; a program needn't handle non-finite values.
Results may differ from a plain program's by a relative error of at most 0.0014.
Values may be sent and summed in bfloat16 or wider, within the bound.
No kernel may reach another device: no remote copies, remote signals or barrier semaphores. Data moves between devices by JAX's collectives and lax.ppermute only.
A program may use at most 576 MiB of HBM per device.

v0:
```python
import jax
import jax.numpy as jnp
from jax import lax
from jax.experimental import pallas as pl
from jax.experimental.pallas import tpu as pltpu
from jax.sharding import PartitionSpec as P

EDGE = 16
CAP = 8
BRICK = 4096
SLOTS = 72
KAPPA = 32.0
OMEGA = 0.8
KEEP = 1.0 - OMEGA

C = 32
NT = 8
F32 = jnp.float32
BF16 = jnp.bfloat16


def spread(level):
    return KAPPA / 4.0**level


def shifted(values, distance, axis):
    return pltpu.roll(values, distance % values.shape[axis], axis)


def iota(shape, dim):
    return lax.broadcasted_iota(jnp.int32, shape, dim)


def lanes(t):
    return slice(t * 128, (t + 1) * 128)


def plane(ref, p):
    count = ref.shape[2] // 128
    rows = ref.shape[1]
    lane = iota((rows, 128), 1)
    before, here = None, ref[p, :, lanes(0)]
    for t in range(count):
        after = ref[p, :, lanes(t + 1)] if t + 1 < count else None
        low = jnp.where(lane == 127, 0.0 if before is None else before, here)
        high = jnp.where(lane == 0, 0.0 if after is None else after, here)
        sums = shifted(low, 1, 1) + shifted(high, -1, 1)
        sums = sums + (shifted(here, 1, 0) + shifted(here, -1, 0))
        sums = sums + (ref[p - 1, :, lanes(t)] + ref[p + 1, :, lanes(t)])
        yield t, here, sums
        before, here = here, after


def loop(start, stop, body, unroll=1):
    def step(i, carry):
        body(i)
        return carry

    lax.fori_loop(start, stop, step, 0, unroll=unroll)


def split_dot(a, b):
    high = a.astype(BF16)
    low = (a - high.astype(F32)).astype(BF16)
    return jnp.dot(high, b, preferred_element_type=F32) + jnp.dot(low, b, preferred_element_type=F32)


def pooling():
    return jnp.where(iota((256, 128), 0) // 2 == iota((256, 128), 1), 0.125, 0.0).astype(BF16)


def doubling():
    return jnp.where(iota((128, 256), 1) // 2 == iota((128, 256), 0), 1.0, 0.0).astype(BF16)


def halve_rows(values, rs, t):
    rows = values.shape[0]
    rs[t, 0:rows, :] = values
    return rs[t, pl.ds(0, rows // 2, stride=2), :] + rs[t, pl.ds(1, rows // 2, stride=2), :]


def halve_lanes(xp, planes, rows):
    matrix = pooling()
    tiles = []
    for t in range(0, xp.shape[0], 2):
        pair = jnp.concatenate([xp[t].reshape(planes * rows, 128), xp[t + 1].reshape(planes * rows, 128)], axis=1)
        tiles.append(split_dot(pair, matrix).reshape(planes, rows, 128))
    return tiles


def inside(shape, dim, first, wrap, index, size, count):
    place = iota(shape, dim) + first
    if wrap is not None:
        place = jnp.where(place < wrap, place, place - shape[dim])
    place = place + index * size
    return (place >= 0) & (place < count * size)


BLOCK = 272
X_ROWS = BLOCK + 3 * 64
Z_ROWS = BLOCK + 5 * 64


def uptake_part(t):
    return slice(BLOCK + 64 * (t // 3), BLOCK + 64 * (t // 3) + 64), lanes(t % 3)


def transposed_bricks(bricks_x, ids, counts, bricks, xs, targets):
    xs[...] = bricks[...].astype(F32)
    row = iota((1, 8, 128), 1)
    group = iota((1, 8, 128), 2) // 16
    group16 = iota((16, 128), 1) // 16
    per_y = 64

    def block(j, out, part):
        start = pl.multiple_of(j * 8, 8)
        x = jnp.stack([xs[pl.ds(start, 8), lanes(k)] for k in range(32)])
        for s in (4, 2, 1):
            up = shifted(shifted(x, -s, 1), 16 * s, 2)
            down = shifted(shifted(x, s, 1), -16 * s, 2)
            row_bit = (row // s) % 2
            group_bit = (group // s) % 2
            x = jnp.where(row_bit == group_bit, x, jnp.where(row_bit == 0, up, down))
        x = jnp.where(group < counts[0, j], x, 0.0)
        out[0:256, part] = x.reshape(256, 128).astype(BF16)
        names = jnp.zeros((16, 128), jnp.int32)
        for e in range(CAP):
            number = ids[j * 8 + e]
            by = lax.rem(number, per_y)
            rest = lax.div(number, per_y)
            bx = lax.rem(rest, 2)
            bz = lax.rem(lax.div(rest, bricks_x), 2)
            names = jnp.where(group16 == e, (bz * 2 + bx) * per_y + by, names)
        out[256:272, part] = names.astype(F32).astype(BF16)

    for i, out in enumerate(targets):
        for d in range(3):
            block(3 * i + d, out, lanes(d))


def first_kernel(bricks_x, ids, counts, bricks, uptake_in, own, r1, r2, zl, zh, xl, xh, rs, xp, rs1, xp1, xs, uptake, sems):
    load = pltpu.make_async_copy(uptake_in, uptake, sems.at[0])
    load.start()
    transposed_bricks(bricks_x, ids, counts, bricks, xs, (zl, own, zh))
    load.wait()

    def pair(m):
        for t in range(NT):
            both = uptake[2 * m, :, lanes(t)] + uptake[2 * m + 1, :, lanes(t)]
            xp[t, m] = halve_rows(both, rs, t)

    loop(0, 16, pair)
    for t, tile in enumerate(halve_lanes(xp, 16, 16)):
        r1[:, :, lanes(t)] = tile

    def pair1(m):
        for t in range(4):
            both = r1[2 * m, :, lanes(t)] + r1[2 * m + 1, :, lanes(t)]
            xp1[t, m] = halve_rows(both, rs1, t)

    loop(0, 8, pair1)
    for t, tile in enumerate(halve_lanes(xp1, 8, 8)):
        r2[:, lanes(t)] = tile.reshape(64, 128)
    for ref, u, r in ((zl, slice(0, 2), slice(0, 4)), (zh, slice(30, 32), slice(12, 16))):
        for t in range(8):
            ref[uptake_part(t)] = uptake[u, :, lanes(t)].reshape(64, 128).astype(BF16)
        for t in range(4):
            ref[uptake_part(8 + t)] = r1[r, :, lanes(t)].reshape(64, 128).astype(BF16)
        for t in range(2):
            ref[uptake_part(12 + t)] = r2[:, lanes(t)].astype(BF16)
        ref[uptake_part(14)] = jnp.zeros((64, 128), BF16)

    sub = iota((8, 1024), 0)

    def columns(i):
        lows, highs = [], []
        for j in range(2):
            low, high = jnp.zeros((8, 1024), F32), jnp.zeros((8, 1024), F32)
            for n in range(4):
                z = 8 * i + 4 * j + n
                low = jnp.where(sub // 2 == n, shifted(uptake[z, 0:8, :], 2 * n, 0), low)
                high = jnp.where(sub // 2 == n, shifted(uptake[z, 24:32, :], 2 * n + 2, 0), high)
            lows.append(low)
            highs.append(high)
        rows = pl.ds(pl.multiple_of(16 * i, 16), 16)
        xl[rows, :] = jnp.concatenate(lows, axis=0).astype(BF16)
        xh[rows, :] = jnp.concatenate(highs, axis=0).astype(BF16)

    loop(0, 4, columns)


def far_along_z(nz, iz, to_low, to_high):
    if nz != 4:
        return to_low, to_high
    one = jnp.where(iz < 2, to_high, to_low)
    return one, one


def halves(sub, first, second):
    return jnp.where(sub < 4, first, shifted(second, 4, 1))


def uppers(sub, first, second):
    return jnp.where(sub < 4, shifted(first, 4, 1), second)


def far_messages(window):
    planes, _, width = window.shape
    pairs = window.reshape(planes // 2, 2, 8, width)
    sub = iota((planes // 2, 8, width), 1)
    size = (planes * 4, width)
    return halves(sub, pairs[:, 0], pairs[:, 1]).reshape(size), uppers(sub, pairs[:, 0], pairs[:, 1]).reshape(size)


def far_tile(from_low, from_high):
    width = from_low.shape[-1]
    low, high = from_low.reshape(-1, 8, width), from_high.reshape(-1, 8, width)
    sub = iota(low.shape, 1)
    even = jnp.where(sub < 4, high, shifted(low, 4, 1))
    odd = jnp.where(sub < 4, shifted(high, 4, 1), low)
    return jnp.stack([even, odd], axis=1).reshape(-1, 8, width)


def first_x_kernel(own, r1, uxl, uxh, zl, zh, q1, xl, xh):
    q1[4:20] = r1[...]
    for ref, planes in ((zl, slice(0, 4)), (zh, slice(20, 24))):
        for t in range(4):
            q1[planes, :, lanes(t)] = ref[uptake_part(8 + t)].astype(F32).reshape(4, 16, 128)
    for ref, d in ((xl, 0), (xh, 2)):
        for n, src in enumerate((own, zl, zh)):
            ref[0:BLOCK, lanes(n)] = src[0:BLOCK, lanes(d)]
    sub = iota((8, 128), 0)
    lows, highs = [], []
    for t in range(8):
        xl[uptake_part(t)] = uxl[:, lanes(t)]
        xh[uptake_part(t)] = uxh[:, lanes(t)]
        both = [ref[uptake_part(t)].astype(F32) for ref in (zl, zh)]
        planes = [both[0][0:32], both[0][32:64], both[1][0:32], both[1][32:64]]
        to_low, to_high = jnp.zeros((8, 128), F32), jnp.zeros((8, 128), F32)
        for n, p in enumerate(planes):
            here = sub // 2 == n
            to_low = jnp.where(here, shifted(p[0:8], 2 * n, 0), to_low)
            to_high = jnp.where(here, shifted(p[24:32], 2 * n + 2, 0), to_high)
        lows.append(to_low)
        highs.append(to_high)
    xl[uptake_part(8)] = jnp.concatenate(lows, axis=0).astype(BF16)
    xh[uptake_part(8)] = jnp.concatenate(highs, axis=0).astype(BF16)


FAR = 80


def source_window_kernel(nz, own, zl, zh, z2l, z2h, r2, firstl, firsth, f2, q2, nl, nh, fl, fh):
    iz = lax.axis_index("gz")
    zeros = jnp.zeros((10, 8, 256), F32)
    f2[0:10] = zeros
    f2[22:32] = zeros
    f2[10:22] = own[...].reshape(12, 8, 256)
    for ref, planes in ((zl, slice(2, 14)), (zh, slice(18, 30))):
        part = jnp.concatenate([ref[240:288, 0:256], ref[240:288, 256:512]], axis=0).astype(F32)
        f2[planes] = f2[planes] + part.reshape(12, 8, 256)
    for ref, planes, exists in ((z2l, slice(0, 6), iz >= 2), (z2h, slice(26, 32), iz < nz - 2)):
        part = jnp.where(exists, ref[0:48, :].astype(F32), 0.0)
        f2[planes] = f2[planes] + part.reshape(6, 8, 256)
    q2[0:4] = z2l[48:80, :].astype(F32).reshape(4, 8, 256)
    q2[28:32] = z2h[48:80, :].astype(F32).reshape(4, 8, 256)
    q2[12:20] = r2[...].reshape(8, 8, 256)
    for ref, planes in ((firstl, slice(4, 12)), (firsth, slice(20, 28))):
        for t in range(2):
            q2[planes, :, lanes(t)] = ref[uptake_part(12 + t)].astype(F32).reshape(8, 8, 128)
    for i, near in enumerate((nl, nh)):
        near[0:256, :] = f2[...].reshape(256, 256).astype(BF16)
        near[256:288, :] = z2l[48:80, :]
        near[288:320, :] = z2h[48:80, :]
        for n in range(4):
            rows = slice(288 + 32 * (n // 2) + 16 * i, 304 + 32 * (n // 2) + 16 * i)
            cols = slice(256 * (n % 2), 256 * (n % 2) + 256)
            near[320 + 32 * n : 336 + 32 * n, :] = zl[rows, cols]
            near[336 + 32 * n : 352 + 32 * n, :] = zh[rows, cols]
    for i, ref in enumerate((f2, q2)):
        to_low, to_high = far_messages(ref[...])
        fl[128 * i : 128 * i + 128, :] = to_low.astype(BF16)
        fh[128 * i : 128 * i + 128, :] = to_high.astype(BF16)


O = 5
Q = 2
BASE = 1.0 + 6.0 * KAPPA


def scatter(blocks, hot, left):
    lane = iota((128, 128), 1)
    for i, (ref, part) in enumerate(blocks):
        name = ref[256:272, part].astype(F32).astype(jnp.int32)[0:1]
        tiles = lax.shift_right_logical(name, 6)
        at_y = (name & 63) * 16 + (lane[0:1] & 15)
        at_y = jnp.broadcast_to(at_y.astype(F32), (128, 128)).T.astype(jnp.int32)
        for t in range(NT):
            hot[128 * i : 128 * i + 128, lanes(t)] = jnp.where(at_y == lane + 128 * t, 1.0, 0.0).astype(BF16)
        values = ref[0:256, part].astype(F32)
        for tile in range(4):
            left[256 * tile : 256 * tile + 256, lanes(i)] = jnp.where(tiles == tile, values, 0.0).astype(BF16)
    for n in range(4):
        cols = slice(n * 256, (n + 1) * 256)
        sums = jnp.dot(left[...], hot[:, cols], preferred_element_type=F32)
        for tile in range(4):
            bz, bx = tile // 2, tile % 2
            yield 16 * bz, slice(16 * bx, 16 * bx + 16), cols, sums[256 * tile : 256 * tile + 256].reshape(16, 16, 256)


def sweep(src, dst, source, gg, z, sourced):
    for t, here, sums in plane(src, z + O):
        inner = KAPPA * sums
        g = gg[z + Q, :, lanes(t)]
        if sourced:
            body = inner[0:32] + source[z, :, lanes(t)]
            dst[z + O, 0:32, lanes(t)] = KEEP * here[0:32] + g[0:32] * body
            dst[z + O, 32:40, lanes(t)] = KEEP * here[32:40] + g[32:40] * inner[32:40]
        else:
            dst[z + O, :, lanes(t)] = KEEP * here + g * inner


def own_kernel(
    nz, own, zl, zh, density, uptake, s_out, g_out, v_out, edge_out,
    dens, upt, s0, g0, v1, edge, va, hot, left, sems,
):
    iz = lax.axis_index("gz")
    loads = [pltpu.make_async_copy(density, dens, sems.at[0]), pltpu.make_async_copy(uptake, upt, sems.at[1])]
    stores = [
        pltpu.make_async_copy(src, dst, sems.at[2 + i])
        for i, (src, dst) in enumerate(((s0, s_out), (g0, g_out), (v1, v_out), (edge, edge_out)))
    ]
    for copy in loads:
        copy.start()
    for p in (3, 4, 37, 38):
        va[p] = jnp.zeros((40, 1024), F32)
    for n in range(4):
        ref, valid = (zl, iz > 0) if n < 2 else (zh, iz < nz - 1)
        q = n if n < 2 else 32 + n
        rows = slice(32 * (n % 2), 32 * (n % 2) + 32)
        for t in range(NT):
            g0[q, :, lanes(t)] = jnp.where(valid, OMEGA, 0.0) / (ref[uptake_part(t)].astype(F32)[rows] + BASE)

    blocks = [(ref, lanes(1)) for ref in (own, zl, zh)]
    waiting = list(loads[0:1])
    for z, rows, cols, sums in scatter(blocks, hot, left):
        while waiting:
            waiting.pop().wait()
        planes = slice(z, z + 16)
        s0[planes, rows, cols] = dens[planes, rows, cols] + sums
    stores[0].start()
    loads[1].wait()

    def own_plane(z):
        va[z + O, 0:32, :] = dens[z]
        va[z + O, 32:40, :] = jnp.zeros((8, 1024), F32)
        g0[z + Q] = OMEGA / (upt[z] + BASE)

    loop(0, C, own_plane)
    stores[1].start()

    def first(z):
        for t, here, sums in plane(va, z + O):
            inner = KAPPA * sums
            body = inner[0:32] + s0[z, :, lanes(t)]
            v1[z + 1, :, lanes(t)] = KEEP * here[0:32] + g0[z + Q, :, lanes(t)] * body
            edge[z, :, lanes(t)] = inner[32:40]

    loop(0, C, first, 2)
    for z in (-1, C):
        for t in range(NT):
            near = va[z + O + (1 if z < 0 else -1), 0:32, lanes(t)]
            v1[z + 1, :, lanes(t)] = g0[z + Q, :, lanes(t)] * (KAPPA * near)
    for copy in stores[2:]:
        copy.start()
    for copy in stores:
        copy.wait()


def pre_kernel(
    nz, nx, xl, xh, zl, zh, q1, s0, g0, v1, edge_in, uptake,
    c1, mxl, mxh, v_out, g_out, s_out,
    va, vb, supply, upt, dh, gg, edge, hot, left, rs, xp, usl, ush, sems,
):
    iz, ix = lax.axis_index("gz"), lax.axis_index("xy")
    k = KAPPA
    loads = [
        pltpu.make_async_copy(src, dst, sems.at[i])
        for i, (src, dst) in enumerate(
            (
                (s0, supply),
                (v1, vb.at[4:38, 0:32, :]),
                (g0, gg.at[:, 0:32, :]),
                (edge_in, edge),
                (uptake, upt),
            )
        )
    ]
    for copy in loads:
        copy.start()

    for p in (1, 2, 39, 40):
        va[p] = jnp.zeros((40, 1024), F32)
    for p in (2, 3, 38, 39):
        vb[p] = jnp.zeros((40, 1024), F32)
    for p in (4, 37):
        vb[p, 32:40, :] = jnp.zeros((8, 1024), F32)

    sub8 = iota((8, 1024), 0)
    for t in range(NT):
        usl[0:64, lanes(t)] = xl[uptake_part(t)].astype(F32)
        ush[0:64, lanes(t)] = xh[uptake_part(t)].astype(F32)
        usl[64:72, lanes(t)] = xl[uptake_part(8)].astype(F32)[8 * t : 8 * t + 8]
        ush[64:72, lanes(t)] = xh[uptake_part(8)].astype(F32)[8 * t : 8 * t + 8]

    def set_halo(q, low, high, valid_z):
        gz = jnp.where(valid_z, OMEGA, 0.0)
        d = jnp.where(sub8 < 2, high, jnp.where(sub8 >= 6, low, 0.0)) + BASE
        dh[q] = d
        omega = jnp.where(sub8 < 2, jnp.where(ix < nx - 1, gz, 0.0), jnp.where(sub8 >= 6, jnp.where(ix > 0, gz, 0.0), 0.0))
        gg[q, 32:40, :] = omega / d

    def halos(i):
        rows = pl.ds(pl.multiple_of(8 * i, 8), 8)
        low, high = usl[rows, :], ush[rows, :]
        for n in range(4):
            set_halo(4 * i + n + Q, shifted(low, 6 - 2 * n, 0), shifted(high, -2 * n, 0), True)

    loop(0, C // 4, halos)
    low, high = usl[64:72, :], ush[64:72, :]
    for n in range(4):
        exists = iz > 0 if n < 2 else iz < nz - 1
        set_halo(n if n < 2 else 32 + n, shifted(low, 6 - 2 * n, 0), shifted(high, -2 * n, 0), exists)

    blocks = [(ref, lanes(n)) for ref in (xl, xh) for n in range(3)]
    waiting = list(loads[0:3])
    for z, rows, cols, sums in scatter(blocks, hot, left):
        while waiting:
            waiting.pop().wait()
        supply[z : z + 16, rows, cols] = supply[z : z + 16, rows, cols] + sums
        g = gg[z + Q : z + Q + 16, rows, cols]
        vb[z + O : z + O + 16, rows, cols] = vb[z + O : z + O + 16, rows, cols] + g * sums
    loads[3].wait()

    s_copy = pltpu.make_async_copy(supply, s_out, sems.at[7])
    s_copy.start()

    def edges(z):
        vb[z + O, 32:40, :] = gg[z + Q, 32:40, :] * edge[z]

    loop(0, C, edges)

    loop(0, C, lambda z: sweep(vb, va, supply, gg, z, True), 2)
    loop(0, 4, lambda i: sweep(vb, va, supply, gg, jnp.where(i < 2, i - 2, i + C - 2), False))
    loads[4].wait()
    v_copy = pltpu.make_async_copy(va.at[3:39], v_out, sems.at[5])
    g_copy = pltpu.make_async_copy(gg, g_out, sems.at[6])
    v_copy.start()
    g_copy.start()

    def residual(z, rates, sourced):
        for t, here, sums in plane(va, z + O):
            r = k * sums
            if rates is not None:
                inner = r[0:32] - (rates(t) + BASE) * here[0:32]
                if sourced:
                    inner = inner + supply[z, :, lanes(t)]
                r = jnp.concatenate([inner, r[32:40] - dh[z + Q, :, lanes(t)] * here[32:40]], axis=0)
            yield t, r

    def coarse(m, zs, rates, sourced):
        parts = [residual(zs[i], rates[i], sourced) for i in range(2)]
        for (t, first), (_, second) in zip(*parts):
            xp[t, m, 0:20, :] = halve_rows(first + second, rs, t)

    def from_message(ref, n):
        return lambda t: ref[uptake_part(t)].astype(F32)[32 * n : 32 * n + 32]

    def inner(m):
        zs = (2 * m - 4, 2 * m - 3)
        coarse(m, zs, [lambda t, z=z: upt[z, :, lanes(t)] for z in zs], True)

    loop(2, 18, inner)
    for m, ref, z in ((1, zl, -2), (18, zh, C)):
        coarse(m, (z, z + 1), [from_message(ref, 0), from_message(ref, 1)], False)

    def outer(i):
        for t, r in residual(jnp.where(i == 0, -3, 34), None, False):
            xp[t, 19 * i, 0:20, :] = halve_rows(r, rs, t)

    loop(0, 2, outer)

    sub = iota((20, 8, 128), 1)
    for t, tile in enumerate(halve_lanes(xp, 20, 24)):
        last = tile[:, 16:24]
        last = jnp.where(sub < 2, last, jnp.where(sub >= 6, shifted(last, 4, 1), 0.0))
        c1[:, 0:16, lanes(t)] = tile[:, 0:16]
        c1[:, 16:24, lanes(t)] = last

    sub1 = iota((5, 8, 512), 1)
    first, last, halo = [c1[:, 8 * n : 8 * n + 8].reshape(5, 4, 8, 512) for n in range(3)]
    sub4 = iota((5, 4, 8, 512), 2)
    to_high = in_three(sub1, jnp.where(sub4 >= 4, last, halo), *HIGH_PACK)
    to_low = in_three(sub1, jnp.where(sub4 >= 4, halo, first), *LOW_PACK)
    sub1 = iota((12, 8, 512), 1)
    first = q1[:, 0:8, :].reshape(12, 2, 8, 512)
    last = q1[:, 8:16, :].reshape(12, 2, 8, 512)
    low_rates = halves(sub1, first[:, 0], first[:, 1]).reshape(96, 512)
    high_rates = uppers(sub1, last[:, 0], last[:, 1]).reshape(96, 512)
    filler = jnp.zeros((8, 512), F32)
    for ref, sources, rates in ((mxl, to_low, low_rates), (mxh, to_high, high_rates)):
        ref[0:128, :] = jnp.concatenate([sources.reshape(120, 512), filler], axis=0).astype(BF16)
        ref[128:224, :] = rates.astype(BF16)

    v_copy.wait()
    g_copy.wait()
    s_copy.wait()


def edges_kernel(r2, zl, zh, v_in, s_in, vzl, vzh, pxl, pxh, cnl, cnh, vx, vz, sx, sz, sems):
    copies = [
        (v_in.at[:, 0:8, :], vx.at[:, 0:8, :]),
        (v_in.at[:, 24:40, :], vx.at[:, 8:24, :]),
        (v_in.at[0:4], vz.at[0]),
        (v_in.at[32:36], vz.at[1]),
        (s_in.at[:, 0:8, :], sx.at[:, 0:8, :]),
        (s_in.at[:, 24:32, :], sx.at[:, 8:16, :]),
        (s_in.at[0], sz.at[0]),
        (s_in.at[31], sz.at[1]),
    ]
    copies = [pltpu.make_async_copy(src, dst, sems.at[i]) for i, (src, dst) in enumerate(copies)]
    for copy in copies:
        copy.start()
    sub8 = iota((8, 1024), 0)
    for ref in (pxl, pxh):
        for t in range(2):
            ref[176:240, lanes(t)] = zl[uptake_part(12 + t)]
            ref[176:240, lanes(2 + t)] = r2[:, lanes(t)].astype(BF16)
            ref[176:240, lanes(4 + t)] = zh[uptake_part(12 + t)]
        ref[176:240, 768:1024] = jnp.zeros((64, 256), BF16)
    for copy in copies:
        copy.wait()

    for i, (level0, corners) in enumerate(((vzl, cnl), (vzh, cnh))):
        level0[0:160, :] = vz[i].reshape(160, 1024).astype(BF16)
        last = jnp.concatenate([sz[i], jnp.zeros((16, 1024), F32)], axis=0)
        level0[160:208, :] = last.astype(BF16)
        planes = [vz[i, n] for n in range(4)]
        low = [pack_low((v[0:8], v[32:40]), (w[0:8], w[32:40])) for v, w in (planes[0:2], planes[2:4])]
        high = [pack_high((v[24:32], v[32:40]), (w[24:32], w[32:40])) for v, w in (planes[0:2], planes[2:4])]
        corners[...] = jnp.concatenate(low + high, axis=0).astype(BF16)

    def sides(i):
        lows, highs = [], []
        for j in range(2):
            p = 4 * i + 2 * j
            v, w = vx[p], vx[p + 1]
            lows.append(pack_low((v[0:8], v[16:24]), (w[0:8], w[16:24])))
            highs.append(pack_high((v[8:16], v[16:24]), (w[8:16], w[16:24])))
        rows = pl.ds(pl.multiple_of(16 * i, 16), 16)
        pxl[rows, :] = jnp.concatenate(lows, axis=0).astype(BF16)
        pxh[rows, :] = jnp.concatenate(highs, axis=0).astype(BF16)

    loop(0, 9, sides)

    def sources(i):
        lows, highs = [], []
        for j in range(2):
            low, high = jnp.zeros((8, 1024), F32), jnp.zeros((8, 1024), F32)
            for n in range(8):
                z = 16 * i + 8 * j + n
                low = jnp.where(sub8 == n, shifted(sx[z, 0:8, :], n, 0), low)
                high = jnp.where(sub8 == n, shifted(sx[z, 8:16, :], n + 1, 0), high)
            lows.append(low)
            highs.append(high)
        rows = pl.ds(pl.multiple_of(16 * i + 144, 16), 16)
        pxl[rows, :] = jnp.concatenate(lows, axis=0).astype(BF16)
        pxh[rows, :] = jnp.concatenate(highs, axis=0).astype(BF16)

    loop(0, 2, sources)


def outer_rows(sub):
    return (sub < 2) | (sub >= 6)


def pack_pair(sub, a, b):
    return jnp.where(outer_rows(sub), a, shifted(b, 4, 0))


def pack_low(first, second):
    sub = iota((8, 1024), 0)
    a, b = [jnp.where(sub < 4, near, halo) for near, halo in (first, second)]
    return pack_pair(sub, a, b)


def pack_high(first, second):
    sub = iota((8, 1024), 0)
    a, b = [jnp.where(sub >= 4, near, halo) for near, halo in (first, second)]
    return pack_pair(sub, a, b)


def in_three(sub, tiles, free, turns):
    spare = (sub == free) | (sub == free + 1)
    last = tiles[:, 3]
    parts = [jnp.where(spare, shifted(last, turn, 1), tiles[:, i]) for i, turn in enumerate(turns)]
    return jnp.stack(parts, axis=1)


def out_of_three(sub, parts, free, turns):
    last = None
    for i, turn in enumerate(turns):
        back = shifted(parts[:, i], -turn, 1)
        home = (free - turn) % 8
        here = (sub == home) | (sub == home + 1)
        last = jnp.where(here, back, 0.0 if last is None else last)
    return jnp.stack([parts[:, 0], parts[:, 1], parts[:, 2], last], axis=1)


HIGH_PACK = (2, (-2, 4, 2))
LOW_PACK = (4, (-2, 4, 2))


def middle_kernel(nz, nx, c1, q_in, r2, cnl, cnh, mxl, mxh, f1, g1, v1, g2, z1l, z1h, z2l, z2h, q0, va, vv, rs, xp):
    iz, ix = lax.axis_index("gz"), lax.axis_index("xy")
    k = spread(1)
    base = 1.0 + 6.0 * k
    sub5 = iota((5, 8, 512), 1)
    low = out_of_three(sub5, mxl[0:128, :].astype(F32)[0:120].reshape(5, 3, 8, 512), *HIGH_PACK).reshape(20, 8, 512)
    high = out_of_three(sub5, mxh[0:128, :].astype(F32)[0:120].reshape(5, 3, 8, 512), *LOW_PACK).reshape(20, 8, 512)
    sub = iota((20, 8, 512), 1)
    for p in (0, 1, 22, 23):
        f1[p] = jnp.zeros((24, 512), F32)
    f1[2:22, 0:8] = c1[:, 0:8] + jnp.where(sub < 2, low, 0.0)
    f1[2:22, 8:16] = c1[:, 8:16] + jnp.where(sub >= 6, high, 0.0)
    f1[2:22, 16:24] = c1[:, 16:24] + jnp.where(sub >= 4, low, high)
    low, high = [ref[128:224, :].astype(F32).reshape(12, 8, 512) for ref in (mxl, mxh)]
    sub12 = iota((12, 8, 512), 1)
    even = jnp.where(sub12 >= 4, shifted(low, 4, 1), high)
    odd = jnp.where(sub12 >= 4, low, shifted(high, 4, 1))
    q0[:, 0:16] = q_in[...]
    q0[:, 16:24] = jnp.stack([even, odd], axis=1).reshape(24, 8, 512)
    shape = (24, 24, 128)
    valid = inside(shape, 0, -4, None, iz, 16, nz) & inside(shape, 1, 0, 20, ix, 16, nx)
    for t in range(4):
        g = jnp.where(valid, OMEGA, 0.0) / (q0[:, :, lanes(t)] + base)
        g1[:, :, lanes(t)] = g
        va[:, :, lanes(t)] = g * f1[:, :, lanes(t)]
    for p in (0, 1, 24, 25):
        vv[p] = jnp.zeros((24, 512), F32)

    def sweep(p):
        for t, here, sums in plane(va, p):
            vv[p + 1, :, lanes(t)] = KEEP * here + g1[p, :, lanes(t)] * (f1[p, :, lanes(t)] + k * sums)

    loop(1, 23, sweep, 2)
    v1[...] = vv[1:25]

    def residual(p):
        for t, here, sums in plane(vv, p + 1):
            yield t, f1[p, :, lanes(t)] + k * sums - (q0[p, :, lanes(t)] + base) * here

    def coarse(m):
        for (t, first), (_, second) in zip(residual(2 * m), residual(2 * m + 1)):
            xp[t, m] = halve_rows((first + second)[0:16], rs, t)

    loop(0, 12, coarse)
    for t, tile in enumerate(halve_lanes(xp, 12, 8)):
        g2[:, lanes(t)] = tile.reshape(96, 128)
        for ref in (z1l, z1h):
            ref[240:288, lanes(t)] = tile[0:6].reshape(48, 128).astype(BF16)
            ref[240:288, lanes(2 + t)] = tile[6:12].reshape(48, 128).astype(BF16)
    for ref, corners in ((z1l, cnl), (z1h, cnh)):
        ref[288:320, :] = corners[:, 0:512]
        ref[320:352, :] = corners[:, 512:1024]
    for ref, p in ((z1l, 2), (z1h, 18)):
        ref[0:144, :] = vv[p : p + 6].reshape(144, 512).astype(BF16)
        ref[144:240, :] = f1[p : p + 4].reshape(96, 512).astype(BF16)
    low, high = far_along_z(nz, iz, g2[0:48, :], g2[48:96, :])
    z2l[0:48, :] = low.astype(BF16)
    z2h[0:48, :] = high.astype(BF16)
    low, high = far_along_z(nz, iz, r2[0:32, :], r2[32:64, :])
    z2l[48:80, :] = low.astype(BF16)
    z2h[48:80, :] = high.astype(BF16)


def back_kernel(
    nz, nx, f_in, g1, v1, z1l, z1h, vzl, vzh, vxl_in, vxh_in, own2, n2l, n2h, m2l, m2h, q_own, v_in, g_in, s_in,
    out_hbm,
    f2, q2, h2, a2, b2, rs, xp, xpr, wa, w1, zsl, zsh, vb, ws,
    v2, gg, supply, fsl, fsh, out, f1, vxl, vxh, sems,
):
    iz, ix = lax.axis_index("gz"), lax.axis_index("xy")
    matrix = doubling()
    level0 = [
        pltpu.make_async_copy(src, dst, sems.at[i])
        for i, (src, dst) in enumerate(((v_in, v2), (g_in, gg), (s_in, supply)))
    ]
    for copy in level0:
        copy.start()

    f1[...] = f_in[...]
    wa[...] = v1[...]
    for ref, p in ((z1l, 1), (z1h, 17)):
        wa[p : p + 6] = wa[p : p + 6] + ref[0:144, :].astype(F32).reshape(6, 24, 512)
        f1[p + 1 : p + 5] = f1[p + 1 : p + 5] + ref[144:240, :].astype(F32).reshape(4, 24, 512)

    f2[:, 0:8, :] = own2[...]
    f2[:, 8:16, :] = n2h[0:256, :].astype(F32).reshape(32, 8, 256)
    f2[:, 16:24, :] = far_tile(m2l[0:128, :].astype(F32), m2h[0:128, :].astype(F32))
    f2[:, 24:32, :] = n2l[0:256, :].astype(F32).reshape(32, 8, 256)
    q2[:, 0:8, :] = q_own[...]
    q2[:, 16:24, :] = far_tile(m2l[128:256, :].astype(F32), m2h[128:256, :].astype(F32))
    for ref, rows in ((vxh_in, slice(8, 16)), (vxl_in, slice(24, 32))):
        for n in range(3):
            q2[8 * n + 4 : 8 * n + 12, rows, :] = ref[176:240, n * 256 : n * 256 + 256].astype(F32).reshape(8, 8, 256)
    for ref, rows in ((n2h, slice(8, 16)), (n2l, slice(24, 32))):
        outer = ref[256:320, :].astype(F32).reshape(8, 8, 256)
        q2[0:4, rows, :] = outer[0:4]
        q2[28:32, rows, :] = outer[4:8]

    k = spread(2)
    base = 1.0 + 6.0 * k
    shape = (32, 32, 128)
    valid = inside(shape, 0, -12, None, iz, 8, nz) & inside(shape, 1, 0, 20, ix, 8, nx)
    for t in range(2):
        g = jnp.where(valid, OMEGA, 0.0) / (q2[:, :, lanes(t)] + base)
        h2[:, :, lanes(t)] = g
        a2[:, :, lanes(t)] = g * f2[:, :, lanes(t)]
    b2[0] = a2[0]
    b2[31] = a2[31]

    def sweep2(src, dst):
        def body(p):
            for t, here, sums in plane(src, p):
                dst[p, :, lanes(t)] = KEEP * here + h2[p, :, lanes(t)] * (f2[p, :, lanes(t)] + k * sums)

        return body

    loop(1, 31, sweep2(a2, b2), 2)

    def coarse(m):
        total, rates = [0.0, 0.0], [0.0, 0.0]
        for j in range(2):
            p = 2 * m + j
            for t, here, sums in plane(b2, p):
                r = f2[p, :, lanes(t)] + k * sums - (q2[p, :, lanes(t)] + base) * here
                total[t] = total[t] + r
                rates[t] = rates[t] + q2[p, :, lanes(t)]
        for t in range(2):
            xp[t, m] = halve_rows(total[t], rs, t)
            xpr[t, m] = halve_rows(rates[t], rs, t + 2)

    for t in range(2):
        for m in (0, 15):
            xp[t, m] = jnp.zeros((16, 128), F32)
            xpr[t, m] = jnp.zeros((16, 128), F32)
    loop(1, 15, coarse)

    shape = (16, 16, 128)
    valid = inside(shape, 0, -6, None, iz, 4, nz) & inside(shape, 1, 0, 10, ix, 4, nx)
    k3 = spread(3)
    (source,) = halve_lanes(xp, 16, 16)
    (rates,) = halve_lanes(xpr, 16, 16)
    g = jnp.where(valid, OMEGA, 0.0) / (rates + (1.0 + 6.0 * k3))
    v = g * source
    lane = iota(shape, 2)
    for repeat in range(3):
        edge = jnp.zeros((1, 16, 128), F32)
        sums = jnp.concatenate([v[1:], edge], axis=0) + jnp.concatenate([edge, v[:-1]], axis=0)
        sums = sums + shifted(v, 1, 1) + shifted(v, -1, 1)
        sums = sums + jnp.where(lane == 0, 0.0, shifted(v, 1, 2)) + jnp.where(lane == 127, 0.0, shifted(v, -1, 2))
        v = KEEP * v + g * (source + k3 * sums)

    wide = split_dot(v[4:12].reshape(128, 128), matrix).reshape(8, 16, 256)
    for m in range(8):
        for t in range(2):
            part = wide[m, :, lanes(t)]
            rs[t, pl.ds(0, 16, stride=2), :] = part
            rs[t, pl.ds(1, 16, stride=2), :] = part
            for j in range(2):
                p = 8 + 2 * m + j
                b2[p, :, lanes(t)] = b2[p, :, lanes(t)] + rs[t, 0:32, :]
    loop(9, 23, sweep2(b2, a2), 2)
    loop(10, 22, sweep2(a2, b2), 2)

    w = b2[10:22]
    near, far = w[:, 8:16], w[:, 24:32]
    near = jnp.where(iota((12, 8, 256), 1) < 2, near, shifted(far, 4, 1))
    w = jnp.concatenate([w[:, 0:8], near], axis=1).reshape(192, 256)
    wide = [split_dot(w[:, lanes(t)], matrix) for t in range(2)]
    wide = jnp.concatenate(wide, axis=1).reshape(12, 16, 512)
    for m in range(12):
        for t in range(4):
            part = wide[m, :, lanes(t)]
            rs[t, pl.ds(0, 16, stride=2), :] = part
            rs[t, pl.ds(1, 16, stride=2), :] = part
            for j in range(2):
                p = 2 * m + j
                wa[p, :, lanes(t)] = wa[p, :, lanes(t)] + rs[t, 0:24, :]
    k1 = spread(1)

    def sweep1(src, dst):
        def body(p):
            for t, here, sums in plane(src, p):
                dst[p, :, lanes(t)] = KEEP * here + g1[p, :, lanes(t)] * (f1[p, :, lanes(t)] + k1 * sums)

        return body

    loop(2, 22, sweep1(wa, w1), 2)
    loop(3, 21, sweep1(w1, wa), 2)

    sub = iota((18, 8, 128), 1)
    for t in range(4):
        halo = wa[3:21, 16:24, lanes(t)]
        halo = jnp.where(sub < 2, halo, shifted(halo, 4, 1))
        w = jnp.concatenate([wa[3:21, 0:16, lanes(t)], halo], axis=1)
        ws[:, :, t * 256 : t * 256 + 256] = split_dot(w.reshape(432, 128), matrix).reshape(18, 24, 256)

    for copy in level0:
        copy.wait()
    zsl[...] = vzl[...].astype(F32)
    zsh[...] = vzh[...].astype(F32)
    for ref, src, near in ((vxl, vxl_in, n2l), (vxh, vxh_in, n2h)):
        ref[...] = src[0:176, :]
        for n in range(4):
            cols = slice(256 * n, 256 * n + 256)
            for i, rows in enumerate((slice(0, 16), slice(128, 144))):
                corner = near[320 + 32 * n + 16 * i : 336 + 32 * n + 16 * i, :].astype(F32)
                ref[rows, cols] = (src[rows, cols].astype(F32) + corner).astype(BF16)
    for i in range(4):
        v2[i] = v2[i] + zsl[40 * i : 40 * i + 40, :]
        v2[32 + i] = v2[32 + i] + zsh[40 * i : 40 * i + 40, :]

    s8 = iota((8, 128), 0)

    outer = outer_rows(s8)

    def correct(i):
        rows = pl.ds(pl.multiple_of(16 * i, 16), 16)
        for t in range(NT):
            low = vxl[rows, lanes(t)].astype(F32)
            high = vxh[rows, lanes(t)].astype(F32)
            for n in range(2):
                part = ws[2 * i + n, :, lanes(t)]
                rs[t, pl.ds(0, 24, stride=2), :] = part
                rs[t, pl.ds(1, 24, stride=2), :] = part
                for j in range(2):
                    p = 4 * i + 2 * n + j
                    lo, hi = low[8 * n : 8 * n + 8], high[8 * n : 8 * n + 8]
                    if j:
                        lo, hi = shifted(lo, 4, 0), shifted(hi, 4, 0)
                    v2[p, 0:8, lanes(t)] = v2[p, 0:8, lanes(t)] + rs[t, 0:8, :] + jnp.where(s8 < 2, lo, 0.0)
                    v2[p, 8:24, lanes(t)] = v2[p, 8:24, lanes(t)] + rs[t, 8:24, :]
                    v2[p, 24:32, lanes(t)] = v2[p, 24:32, lanes(t)] + rs[t, 24:32, :] + jnp.where(s8 >= 6, hi, 0.0)
                    extra = jnp.where(outer, jnp.where(s8 >= 4, lo, hi), 0.0)
                    v2[p, 32:40, lanes(t)] = v2[p, 32:40, lanes(t)] + rs[t, 32:40, :] + extra

    loop(0, 9, correct)
    k0 = spread(0)

    def first(i):
        rows = pl.ds(pl.multiple_of(16 * i + 144, 16), 16)
        for t in range(NT):
            fsl[:, lanes(t)] = vxl[rows, lanes(t)].astype(F32)
            fsh[:, lanes(t)] = vxh[rows, lanes(t)].astype(F32)

        def step(j):
            z = 16 * i + j
            start = pl.multiple_of((j // 8) * 8, 8)
            turn = lax.rem(j, 8)
            for t, here, sums in plane(v2, z + 2):
                lo = pltpu.roll(fsl[pl.ds(start, 8), lanes(t)], 7 - turn, 0)
                hi = pltpu.roll(fsh[pl.ds(start, 8), lanes(t)], lax.rem(8 - turn, 8), 0)
                f = jnp.where(s8 == 7, lo, jnp.where(s8 == 0, hi, 0.0))
                g = gg[z + 2, :, lanes(t)]
                inner = k0 * sums
                vb[z + 1, 0:32, lanes(t)] = KEEP * here[0:32] + g[0:32] * (supply[z, :, lanes(t)] + inner[0:32])
                vb[z + 1, 32:40, lanes(t)] = KEEP * here[32:40] + g[32:40] * (f + inner[32:40])

        loop(0, 16, step, 2)

    loop(0, 2, first)
    for p, ref in ((1, zsl), (34, zsh)):
        for t, here, sums in plane(v2, p):
            g = gg[p, :, lanes(t)]
            vb[p - 1, :, lanes(t)] = KEEP * here + g * (ref[160:200, lanes(t)] + k0 * sums)

    def second(z):
        for t, here, sums in plane(vb, z + 1):
            g = gg[z + 2, 0:32, lanes(t)]
            out[z, :, lanes(t)] = KEEP * here[0:32] + g * (supply[z, :, lanes(t)] + k0 * sums[0:32])

    stores = []
    for i in range(4):
        part = pl.ds(8 * i, 8)
        loop(8 * i, 8 * i + 8, second, 2)
        stores.append(pltpu.make_async_copy(out.at[part], out_hbm.at[part], sems.at[3 + i]))
        stores[i].start()
    for copy in stores:
        copy.wait()


VMEM = pl.BlockSpec(memory_space=pltpu.VMEM)
SMEM = pl.BlockSpec(memory_space=pltpu.SMEM)
ANY = pl.BlockSpec(memory_space=pl.ANY)


def call(kernel, outs, scratch, smem, args, out_specs=None, in_hbm=0):
    moved = sum(a.size * a.dtype.itemsize for a in list(args) + list(outs))
    return pl.pallas_call(
        kernel,
        out_shape=tuple(outs),
        in_specs=[SMEM] * smem + [VMEM] * (len(args) - smem - in_hbm) + [ANY] * in_hbm,
        out_specs=tuple(out_specs or [VMEM] * len(outs)),
        scratch_shapes=scratch,
        compiler_params=pltpu.CompilerParams(vmem_limit_bytes=58 * 2**20),
        cost_estimate=pl.CostEstimate(flops=20 * moved, bytes_accessed=moved, transcendentals=0),
    )(*args)


def shaped(shape, dtype=F32):
    return jax.ShapeDtypeStruct(shape, dtype)


def both_ways(to_low, to_high, axis, distance=1):
    count = lax.axis_size(axis)
    up = [(i, i + distance) for i in range(count - distance)]
    down = [(j, i) for i, j in up]
    return lax.ppermute(to_high, axis, up), lax.ppermute(to_low, axis, down)


def two_away(to_low, to_high):
    count = lax.axis_size("gz")
    if count != 4:
        return both_ways(to_low, to_high, "gz", 2)
    came = lax.ppermute(to_low, "gz", [(i, (i + 2) % 4) for i in range(4)])
    return came, came


def shards(density, uptake, brick_values, brick_ids, slot_counts):
    nz, nx = lax.axis_size("gz"), lax.axis_size("xy")
    scratch = pltpu.VMEM
    half = lambda *shape: shaped(shape, BF16)
    full = lambda *shape: shaped(shape, F32)

    own, r1, r2, zl, zh, uxl, uxh = call(
        lambda *refs: first_kernel(2 * nx, *refs),
        [
            half(BLOCK, 384), full(16, 16, 512), full(64, 256), half(Z_ROWS, 384), half(Z_ROWS, 384),
            half(64, 1024), half(64, 1024),
        ],
        [
            scratch((8, 32, 128), F32), scratch((8, 16, 16, 128), F32), scratch((4, 16, 128), F32),
            scratch((4, 8, 8, 128), F32), scratch((SLOTS, BRICK), F32), scratch((C, C, 1024), F32),
            pltpu.SemaphoreType.DMA((1,)),
        ],
        2,
        (brick_ids, slot_counts, brick_values, uptake),
        in_hbm=1,
    )
    zl, zh = both_ways(zl, zh, "gz")
    q1, xl, xh = call(
        first_x_kernel,
        [full(24, 16, 512), half(X_ROWS, 384), half(X_ROWS, 384)],
        [],
        0,
        (own, r1, uxl, uxh, zl, zh),
    )
    s0, g0, v1, edge = call(
        lambda *refs: own_kernel(nz, *refs),
        [full(C, C, 1024), full(36, C, 1024), full(34, C, 1024), full(C, 8, 1024)],
        [
            scratch((C, C, 1024), F32),
            scratch((C, C, 1024), F32),
            scratch((C, C, 1024), F32),
            scratch((36, C, 1024), F32),
            scratch((34, C, 1024), F32),
            scratch((C, 8, 1024), F32),
            scratch((42, 40, 1024), F32),
            scratch((384, 1024), BF16),
            scratch((1024, 384), BF16),
            pltpu.SemaphoreType.DMA((6,)),
        ],
        0,
        (own, zl, zh, density, uptake),
        [ANY] * 4,
        in_hbm=2,
    )
    xl, xh = both_ways(xl, xh, "xy")

    c1, mxl, mxh, v2, gg, supply = call(
        lambda *refs: pre_kernel(nz, nx, *refs),
        [
            full(20, 24, 512),
            half(224, 512),
            half(224, 512),
            full(36, 40, 1024),
            full(36, 40, 1024),
            full(C, C, 1024),
        ],
        [
            scratch((42, 40, 1024), F32),
            scratch((42, 40, 1024), F32),
            scratch((C, C, 1024), F32),
            scratch((C, C, 1024), F32),
            scratch((36, 8, 1024), F32),
            scratch((36, 40, 1024), F32),
            scratch((C, 8, 1024), F32),
            scratch((768, 1024), BF16),
            scratch((1024, 768), BF16),
            scratch((8, 40, 128), F32),
            scratch((8, 20, 24, 128), F32),
            scratch((72, 1024), F32),
            scratch((72, 1024), F32),
            pltpu.SemaphoreType.DMA((8,)),
        ],
        0,
        (xl, xh, zl, zh, q1, s0, g0, v1, edge, uptake),
        [VMEM] * 3 + [ANY] * 3,
        in_hbm=5,
    )
    mxl, mxh = both_ways(mxl, mxh, "xy")
    vzl, vzh, pxl, pxh, cnl, cnh = call(
        edges_kernel,
        [
            half(208, 1024), half(208, 1024), half(240, 1024), half(240, 1024), half(32, 1024), half(32, 1024),
        ],
        [
            scratch((36, 24, 1024), F32), scratch((2, 4, 40, 1024), F32), scratch((C, 16, 1024), F32),
            scratch((2, C, 1024), F32), pltpu.SemaphoreType.DMA((8,)),
        ],
        0,
        (r2, zl, zh, v2, supply),
        in_hbm=2,
    )
    pxl, pxh, vzl, vzh, c1 = lax.optimization_barrier((pxl, pxh, vzl, vzh, c1))
    pxl, pxh, mxl, mxh = lax.optimization_barrier((pxl, pxh, mxl, mxh))
    vxl, vxh = both_ways(pxl, pxh, "xy")
    f1, g1, v1, g2, z1l, z1h, z2l, z2h = call(
        lambda *refs: middle_kernel(nz, nx, *refs),
        [
            full(24, 24, 512), full(24, 24, 512), full(24, 24, 512), full(96, 256),
            half(352, 512), half(352, 512), half(FAR, 256), half(FAR, 256),
        ],
        [
            scratch((24, 24, 512), F32), scratch((24, 24, 512), F32), scratch((26, 24, 512), F32),
            scratch((4, 16, 128), F32), scratch((4, 12, 8, 128), F32),
        ],
        0,
        (c1, q1, r2, cnl, cnh, mxl, mxh),
    )
    z1l, z1h = both_ways(z1l, z1h, "gz")
    z2l, z2h = two_away(z2l, z2h)
    g2, vxl, vxh = lax.optimization_barrier((g2, vxl, vxh))
    own2, q2, nl, nh, fl, fh = call(
        lambda *refs: source_window_kernel(nz, *refs),
        [full(32, 8, 256), full(32, 8, 256), half(448, 256), half(448, 256), half(256, 256), half(256, 256)],
        [],
        0,
        (g2, z1l, z1h, z2l, z2h, r2, zl, zh),
    )
    vzl, vzh, nl, nh, fl, fh = lax.optimization_barrier((vzl, vzh, nl, nh, fl, fh))
    nl, nh = both_ways(nl, nh, "xy")
    vzl, vzh = both_ways(vzl, vzh, "gz")
    fl, fh = both_ways(fl, fh, "xy", 2)
    window2 = scratch((32, 32, 256), F32)
    window1 = scratch((24, 24, 512), F32)
    (concentration,) = call(
        lambda *refs: back_kernel(nz, nx, *refs),
        [full(C, C, 1024)],
        [
            window2, window2, window2, window2, window2,
            scratch((8, 48, 128), F32),
            scratch((2, 16, 16, 128), F32),
            scratch((2, 16, 16, 128), F32),
            window1, window1,
            scratch((208, 1024), F32),
            scratch((208, 1024), F32),
            scratch((34, 40, 1024), F32),
            scratch((18, 24, 1024), F32),
            scratch((36, 40, 1024), F32),
            scratch((36, 40, 1024), F32),
            scratch((C, C, 1024), F32),
            scratch((16, 1024), F32),
            scratch((16, 1024), F32),
            scratch((C, C, 1024), F32),
            window1,
            scratch((176, 1024), BF16),
            scratch((176, 1024), BF16),
            pltpu.SemaphoreType.DMA((7,)),
        ],
        0,
        (f1, g1, v1, z1l, z1h, vzl, vzh, vxl, vxh, own2, nl, nh, fl, fh, q2, v2, gg, supply),
        [ANY],
        in_hbm=3,
    )
    return supply, concentration


def solution(mesh):
    return jax.shard_map(
        shards,
        mesh=mesh,
        in_specs=(
            P("gz", "xy", None),
            P("gz", "xy", None),
            P(("gz", "xy"), None),
            P(("gz", "xy")),
            P(("gz", "xy"), None),
        ),
        out_specs=(P("gz", "xy", None), P("gz", "xy", None)),
        check_vma=False,
    )
```

profile of v0, /device:TPU:0, one launch (start us, length us, event | category | flops | bytes accessed | tf_op | source)
XLA Modules:
  0.0 157.3 jit_solution(15591133018192260073)
XLA Ops:
  0.6 7.4 %shard_map.68 = (bf16[272,384]{1,0:T(8,128)(2,1)}, f32[16,16,512]{2,1,0:T(8,128)}, f32[64,256]{1,0:T(8,128)}, bf16[592,384]{1,0:T(8,128)(2,1)}, bf16[592,384]{1,...) custom-call(s32[72]{0:T(128)} %refs_0_.1, s32[1,9]{1,0:T(1,128)} %refs_1_.1, ...), custom_call_target="tpu_custom_call" | custom-call | flops 135092560 | bytes 6754628 | tf_op jit(solution)/shard_map/pallas_call | solution.py:911
  8.0 2.4 %collective-permute-start = (bf16[592,384]{1,0:T(8,128)(2,1)}, bf16[592,384]{1,0:T(8,128)(2,1)S(1)}, u32[]{:S(2)}, u32[]{:S(2)}) collective-permute-start(bf16[592,384]{1,0:T(8,128)(2,1)} %get-tuple-element.63), channel_id=1, source_target_pairs={{0,8},{8,16},{16,24},{1,9},{9,17},{17,25},{2,10},{10,18},{18,26},{... | collective-permute-start | bytes 1363976 | tf_op jit(solution)/shard_map/ppermute | solution.py:930
  10.4 1.3 collective-permute-start.1
  12.0 4.4 %collective-permute-done.1.zh.refs_2_.refs_3_.refs_7_ = bf16[592,384]{1,0:T(8,128)(2,1)S(1)} collective-permute-done((bf16[592,384]{1,0:T(8,128)(2,1)}, bf16[592,384]{1,0:T(8,128)(2,1)S(1)}, u32[]{:S(2)}, u32[]{:S(2)}) %collective-permute-start.1) | collective-permute-done | bytes 454688 | tf_op jit(solution)/shard_map/ppermute | solution.py:930
  16.4 0.8 copy-done.1
  17.3 2.6 %shard_map.69 = (f32[24,16,512]{2,1,0:T(8,128)}, bf16[464,384]{1,0:T(8,128)(2,1)}, bf16[464,384]{1,0:T(8,128)(2,1)}) custom-call(bf16[272,384]{1,0:T(8,128)(2,1)} %get-tuple-element.59.own.refs_0_, f32[16,16,512]{2,1,0:T(8,128)} %get-tuple-element.60.r1, bf16[64,1024]{1,0:T(8,128)(2,1)} %get-tuple-element.61.uxl, bf16[64,1024]{1,0:T(8,128)(2,1)} %get-tuple-element.62.uxh, ...), custom_call_target="tpu_custom_call" | custom-call | flops 68075520 | bytes 3403776 | tf_op jit(solution)/shard_map/pallas_call | solution.py:911
  19.9 3.4 %collective-permute-start.2 = (bf16[464,384]{1,0:T(8,128)(2,1)}, bf16[464,384]{1,0:T(8,128)(2,1)S(1)}, u32[]{:S(2)}, u32[]{:S(2)}) collective-permute-start(bf16[464,384]{1,0:T(8,128)(2,1)} %get-tuple-element.65), channel_id=1, source_target_pairs={{0,1},{1,2},{2,3},{3,4},{4,5},{5,6},{6,7},{8,9},{9,10},{10,11},{11... | collective-permute-start | bytes 1069064 | tf_op jit(solution)/shard_map/ppermute | solution.py:930
  23.3 1.3 collective-permute-start.3
  24.6 12.2 %shard_map.70 = (f32[32,32,1024]{2,1,0:T(8,128)}, f32[36,32,1024]{2,1,0:T(8,128)}, f32[34,32,1024]{2,1,0:T(8,128)}, f32[32,8,1024]{2,1,0:T(8,128)}) custom-call(bf16[272,384]{1,0:T(8,128)(2,1)} %get-tuple-element.59.own.refs_0_, bf16[592,384]{1,0:T(8,128)(2,1)} %copy-done, bf16[592,384]{1,0:T(8,128)(2,1)} %copy-done.1, f32[32,32,1024]{2,1,0:T(8,128)} %refs_3_.3, ...), custom_call_target="tpu_custom_call" | custom-call | flops 478494720 | bytes 23924736 | tf_op jit(solution)/shard_map/pallas_call | solution.py:911
  36.9 0.7 copy-done.8
  37.7 20.8 %shard_map.71 = (f32[20,24,512]{2,1,0:T(8,128)}, bf16[224,512]{1,0:T(8,128)(2,1)}, bf16[224,512]{1,0:T(8,128)(2,1)}, f32[36,40,1024]{2,1,0:T(8,128)}, f32[36,40,1024]{2,1,0:T(8,128)}, /*index=5*/f32[32,32,1024]{2,1,0:T(8,128)}) custom-call(bf16[464,384]{1,0:T(8,128)(2,1)} %copy-done.8, bf16[464,384]{1,0:T(8,128)(2,1)} %copy-done.9, ...), custom_call_target="tpu_custom_call" | custom-call | flops 769064960 | bytes 38453248 | tf_op jit(solution)/shard_map/pallas_call | solution.py:911
  58.5 4.6 %collective-permute-start.4 = (bf16[224,512]{1,0:T(8,128)(2,1)}, bf16[224,512]{1,0:T(8,128)(2,1)S(1)}, u32[]{:S(2)}, u32[]{:S(2)}) collective-permute-start(bf16[224,512]{1,0:T(8,128)(2,1)} %get-tuple-element.85), channel_id=1, source_target_pairs={{0,1},{1,2},{2,3},{3,4},{4,5},{5,6},{6,7},{8,9},{9,10},{10,11},{11... | collective-permute-start | bytes 688136 | tf_op jit(solution)/shard_map/ppermute | solution.py:930
  63.1 1.3 collective-permute-start.5
  64.4 6.1 %shard_map.72 = (bf16[208,1024]{1,0:T(8,128)(2,1)}, bf16[208,1024]{1,0:T(8,128)(2,1)}, bf16[240,1024]{1,0:T(8,128)(2,1)}, bf16[240,1024]{1,0:T(8,128)(2,1)}, bf1...) custom-call(f32[64,256]{1,0:T(8,128)} %get-tuple-element.73.r2.refs_2_.refs_5_, bf16[592,384]{1,0:T(8,128)(2,1)} %copy-done, ...), custom_call_target="tpu_custom_call" | custom-call | flops 260669440 | bytes 13033472 | tf_op jit(solution)/shard_map/pallas_call | solution.py:911
  70.6 1.9 %collective-permute-done.5.refs_6_ = bf16[224,512]{1,0:T(8,128)(2,1)S(1)} collective-permute-done((bf16[224,512]{1,0:T(8,128)(2,1)}, bf16[224,512]{1,0:T(8,128)(2,1)S(1)}, u32[]{:S(2)}, u32[]{:S(2)}) %collective-permute-start.5) | collective-permute-done | bytes 229408 | tf_op jit(solution)/shard_map/ppermute | solution.py:930
  72.4 4.9 %collective-permute-start.8 = (bf16[240,1024]{1,0:T(8,128)(2,1)}, bf16[240,1024]{1,0:T(8,128)(2,1)S(1)}, u32[]{:S(2)}, u32[]{:S(2)}) collective-permute-start(bf16[240,1024]{1,0:T(8,128)(2,1)} %get-tuple-element.97), channel_id=1, source_target_pairs={{0,1},{1,2},{2,3},{3,4},{4,5},{5,6},{6,7},{8,9},{9,10},{10,11},{11... | collective-permute-start | bytes 1474568 | tf_op jit(solution)/shard_map/ppermute | solution.py:930
  77.4 1.3 collective-permute-start.9
  78.7 7.3 %shard_map.73 = (f32[24,24,512]{2,1,0:T(8,128)}, f32[24,24,512]{2,1,0:T(8,128)}, f32[24,24,512]{2,1,0:T(8,128)}, f32[96,256]{1,0:T(8,128)}, bf16[352,512]{1,0:T(...) custom-call(f32[20,24,512]{2,1,0:T(8,128)} %get-tuple-element.80.refs_0_, ...), custom_call_target="tpu_custom_call" | custom-call | flops 137297920 | bytes 6864896 | tf_op jit(solution)/shard_map/pallas_call | solution.py:911
  86.0 5.7 %collective-permute-start.6 = (bf16[352,512]{1,0:T(8,128)(2,1)}, bf16[352,512]{1,0:T(8,128)(2,1)S(1)}, u32[]{:S(2)}, u32[]{:S(2)}) collective-permute-start(bf16[352,512]{1,0:T(8,128)(2,1)} %get-tuple-element.92), channel_id=1, source_target_pairs={{0,8},{8,16},{16,24},{1,9},{9,17},{17,25},{2,10},{10,18},{18,26},{... | collective-permute-start | bytes 1081352 | tf_op jit(solution)/shard_map/ppermute | solution.py:930
  91.6 1.5 collective-permute-start.7
  93.1 4.2 %collective-permute-start.10 = (bf16[80,256]{1,0:T(8,128)(2,1)}, bf16[80,256]{1,0:T(8,128)(2,1)S(1)}, u32[]{:S(2)}, u32[]{:S(2)}) collective-permute-start(bf16[80,256]{1,0:T(8,128)(2,1)} %get-tuple-element.100), channel_id=1, source_target_pairs={{0,16},{8,24},{16,0},{24,8},{1,17},{9,25},{17,1},{25,9},{2,18},{10... | collective-permute-start | bytes 122888 | tf_op jit(solution)/shard_map/ppermute | solution.py:937
  97.4 5.9 %collective-permute-done.10.refs_3_.refs_4_ = bf16[80,256]{1,0:T(8,128)(2,1)S(1)} collective-permute-done((bf16[80,256]{1,0:T(8,128)(2,1)}, bf16[80,256]{1,0:T(8,128)(2,1)S(1)}, u32[]{:S(2)}, u32[]{:S(2)}) %collective-permute-start.10) | collective-permute-done | bytes 40992 | tf_op jit(solution)/shard_map/ppermute | solution.py:937
  104.1 0.8 copy-done.3
  104.8 2.5 %shard_map.74 = (f32[32,8,256]{2,1,0:T(8,128)}, f32[32,8,256]{2,1,0:T(8,128)}, bf16[448,256]{1,0:T(8,128)(2,1)}, bf16[448,256]{1,0:T(8,128)(2,1)}, bf16[256,256]{1,0:T(8,128)(2,1)}, /*index=5*/bf16[256,256]{1,0:T(8,128)(2,1)}) custom-call(f32[96,256]{1,0:T(8,128)} %get-tuple-element.99.refs_0_, bf16[352,512]{1,0:T(8,128)(2,1)} %copy-done.2, ...), custom_call_target="tpu_custom_call" | custom-call | flops 62423040 | bytes 3121152 | tf_op jit(solution)/shard_map/pallas_call | solution.py:911
  107.4 1.3 collective-permute-start.11
  108.7 1.3 collective-permute-start.12
  110.0 6.0 %collective-permute-start.15 = (bf16[256,256]{1,0:T(8,128)(2,1)}, bf16[256,256]{1,0:T(8,128)(2,1)S(1)}, u32[]{:S(2)}, u32[]{:S(2)}) collective-permute-start(bf16[256,256]{1,0:T(8,128)(2,1)} %get-tuple-element.112), channel_id=1, source_target_pairs={{0,2},{1,3},{2,4},{3,5},{4,6},{5,7},{8,10},{9,11},{10,12},{11,13},... | collective-permute-start | bytes 393224 | tf_op jit(solution)/shard_map/ppermute | solution.py:930
  116.0 2.0 %collective-permute-start.13 = (bf16[448,256]{1,0:T(8,128)(2,1)}, bf16[448,256]{1,0:T(8,128)(2,1)S(1)}, u32[]{:S(2)}, u32[]{:S(2)}) collective-permute-start(bf16[448,256]{1,0:T(8,128)(2,1)} %get-tuple-element.110), channel_id=1, source_target_pairs={{0,1},{1,2},{2,3},{3,4},{4,5},{5,6},{6,7},{8,9},{9,10},{10,11},{11... | collective-permute-start | bytes 688136 | tf_op jit(solution)/shard_map/ppermute | solution.py:930
  118.0 1.3 collective-permute-start.14
  120.0 1.3 collective-permute-start.16
  121.3 12.1 %collective-permute-done.16.refs_13_ = bf16[256,256]{1,0:T(8,128)(2,1)S(1)} collective-permute-done((bf16[256,256]{1,0:T(8,128)(2,1)}, bf16[256,256]{1,0:T(8,128)(2,1)S(1)}, u32[]{:S(2)}, u32[]{:S(2)}) %collective-permute-start.16) | collective-permute-done | bytes 131104 | tf_op jit(solution)/shard_map/ppermute | solution.py:930
  134.5 22.7 %shard_map.75 = f32[32,32,1024]{2,1,0:T(8,128)} custom-call(f32[24,24,512]{2,1,0:T(8,128)} %get-tuple-element.89.refs_0_, f32[24,24,512]{2,1,0:T(8,128)} %get-tuple-element.90.refs_1_, f32[24,24,512]{2,1,0:T(8,128)} %get-tuple-element.91.refs_2_, bf16[352,512]{1,0:T(8,128)(2,1)} %copy-done.2, bf16[352,512]{1,0:T(8,128)(2,1)} %copy-done.3, ...), custom_call_target="tpu_custom_call" | custom-call | flops 550502400 | bytes 27525120 | tf_op jit(solution)/shard_map/pallas_call | solution.py:911
  (48 shorter events, 3.0 us)
Async XLA Ops:
  8.0 4.0 %collective-permute-start = (bf16[592,384]{1,0:T(8,128)(2,1)}, bf16[592,384]{1,0:T(8,128)(2,1)S(1)}, u32[]{:S(2)}, u32[]{:S(2)}) collective-permute-start(bf16[592,384]{1,0:T(8,128)(2,1)} %get-tuple-element.63), channel_id=1, source_target_pairs={{0,8},{8,16},{16,24},{1,9},{9,17},{17,25},{2,10},{10,18},{18,26},{... | collective-permute-start | bytes 1363976 | tf_op jit(solution)/shard_map/ppermute | solution.py:930
  10.4 6.0 %collective-permute-start.1 = (bf16[592,384]{1,0:T(8,128)(2,1)}, bf16[592,384]{1,0:T(8,128)(2,1)S(1)}, u32[]{:S(2)}, u32[]{:S(2)}) collective-permute-start(bf16[592,384]{1,0:T(8,128)(2,1)} %get-tuple-element.64), channel_id=1, source_target_pairs={{8,0},{16,8},{24,16},{9,1},{17,9},{25,17},{10,2},{18,10},{26,18},{... | collective-permute-start | bytes 1363976 | tf_op jit(solution)/shard_map/ppermute | solution.py:930
  12.0 4.4 %copy-start = (bf16[592,384]{1,0:T(8,128)(2,1)}, bf16[592,384]{1,0:T(8,128)(2,1)S(1)}, u32[]{:S(2)}) copy-start(bf16[592,384]{1,0:T(8,128)(2,1)S(1)} %collective-permute-done.zl.refs_1_.refs_2_.refs_6_) | copy-start | bytes 1363972
  16.4 0.8 copy-start.1
  19.9 16.9 %collective-permute-start.2 = (bf16[464,384]{1,0:T(8,128)(2,1)}, bf16[464,384]{1,0:T(8,128)(2,1)S(1)}, u32[]{:S(2)}, u32[]{:S(2)}) collective-permute-start(bf16[464,384]{1,0:T(8,128)(2,1)} %get-tuple-element.65), channel_id=1, source_target_pairs={{0,1},{1,2},{2,3},{3,4},{4,5},{5,6},{6,7},{8,9},{9,10},{10,11},{11... | collective-permute-start | bytes 1069064 | tf_op jit(solution)/shard_map/ppermute | solution.py:930
  23.3 13.5 %collective-permute-start.3 = (bf16[464,384]{1,0:T(8,128)(2,1)}, bf16[464,384]{1,0:T(8,128)(2,1)S(1)}, u32[]{:S(2)}, u32[]{:S(2)}) collective-permute-start(bf16[464,384]{1,0:T(8,128)(2,1)} %get-tuple-element.66), channel_id=1, source_target_pairs={{1,0},{2,1},{3,2},{4,3},{5,4},{6,5},{7,6},{9,8},{10,9},{11,10},{12... | collective-permute-start | bytes 1069064 | tf_op jit(solution)/shard_map/ppermute | solution.py:930
  36.8 0.9 copy-start.9
  58.5 12.0 %collective-permute-start.4 = (bf16[224,512]{1,0:T(8,128)(2,1)}, bf16[224,512]{1,0:T(8,128)(2,1)S(1)}, u32[]{:S(2)}, u32[]{:S(2)}) collective-permute-start(bf16[224,512]{1,0:T(8,128)(2,1)} %get-tuple-element.85), channel_id=1, source_target_pairs={{0,1},{1,2},{2,3},{3,4},{4,5},{5,6},{6,7},{8,9},{9,10},{10,11},{11... | collective-permute-start | bytes 688136 | tf_op jit(solution)/shard_map/ppermute | solution.py:930
  63.1 9.3 %collective-permute-start.5 = (bf16[224,512]{1,0:T(8,128)(2,1)}, bf16[224,512]{1,0:T(8,128)(2,1)S(1)}, u32[]{:S(2)}, u32[]{:S(2)}) collective-permute-start(bf16[224,512]{1,0:T(8,128)(2,1)} %get-tuple-element.86), channel_id=1, source_target_pairs={{1,0},{2,1},{3,2},{4,3},{5,4},{6,5},{7,6},{9,8},{10,9},{11,10},{12... | collective-permute-start | bytes 688136 | tf_op jit(solution)/shard_map/ppermute | solution.py:930
  70.5 36.8 %copy-start.18 = (bf16[208,1024]{1,0:T(8,128)(2,1)S(1)}, bf16[208,1024]{1,0:T(8,128)(2,1)}, u32[]{:S(2)}) copy-start(bf16[208,1024]{1,0:T(8,128)(2,1)} %get-tuple-element.105) | copy-start | bytes 1277956
  70.5 38.2 %copy-start.17 = (bf16[208,1024]{1,0:T(8,128)(2,1)S(1)}, bf16[208,1024]{1,0:T(8,128)(2,1)}, u32[]{:S(2)}) copy-start(bf16[208,1024]{1,0:T(8,128)(2,1)} %get-tuple-element.106) | copy-start | bytes 1277956
  70.5 8.1 %copy-start.12 = (bf16[224,512]{1,0:T(8,128)(2,1)}, bf16[224,512]{1,0:T(8,128)(2,1)S(1)}, u32[]{:S(2)}) copy-start(bf16[224,512]{1,0:T(8,128)(2,1)S(1)} %collective-permute-done.4.refs_5_) | copy-start | bytes 688132
  72.4 6.3 %copy-start.13 = (bf16[224,512]{1,0:T(8,128)(2,1)}, bf16[224,512]{1,0:T(8,128)(2,1)S(1)}, u32[]{:S(2)}) copy-start(bf16[224,512]{1,0:T(8,128)(2,1)S(1)} %collective-permute-done.5.refs_6_) | copy-start | bytes 688132
  72.4 24.9 %collective-permute-start.8 = (bf16[240,1024]{1,0:T(8,128)(2,1)}, bf16[240,1024]{1,0:T(8,128)(2,1)S(1)}, u32[]{:S(2)}, u32[]{:S(2)}) collective-permute-start(bf16[240,1024]{1,0:T(8,128)(2,1)} %get-tuple-element.97), channel_id=1, source_target_pairs={{0,1},{1,2},{2,3},{3,4},{4,5},{5,6},{6,7},{8,9},{9,10},{10,11},{11... | collective-permute-start | bytes 1474568 | tf_op jit(solution)/shard_map/ppermute | solution.py:930
  77.4 20.0 %collective-permute-start.9 = (bf16[240,1024]{1,0:T(8,128)(2,1)}, bf16[240,1024]{1,0:T(8,128)(2,1)S(1)}, u32[]{:S(2)}, u32[]{:S(2)}) collective-permute-start(bf16[240,1024]{1,0:T(8,128)(2,1)} %get-tuple-element.98), channel_id=1, source_target_pairs={{1,0},{2,1},{3,2},{4,3},{5,4},{6,5},{7,6},{9,8},{10,9},{11,10},{12... | collective-permute-start | bytes 1474568 | tf_op jit(solution)/shard_map/ppermute | solution.py:930
  86.0 17.3 %collective-permute-start.6 = (bf16[352,512]{1,0:T(8,128)(2,1)}, bf16[352,512]{1,0:T(8,128)(2,1)S(1)}, u32[]{:S(2)}, u32[]{:S(2)}) collective-permute-start(bf16[352,512]{1,0:T(8,128)(2,1)} %get-tuple-element.92), channel_id=1, source_target_pairs={{0,8},{8,16},{16,24},{1,9},{9,17},{17,25},{2,10},{10,18},{18,26},{... | collective-permute-start | bytes 1081352 | tf_op jit(solution)/shard_map/ppermute | solution.py:930
  91.6 11.7 %collective-permute-start.7 = (bf16[352,512]{1,0:T(8,128)(2,1)}, bf16[352,512]{1,0:T(8,128)(2,1)S(1)}, u32[]{:S(2)}, u32[]{:S(2)}) collective-permute-start(bf16[352,512]{1,0:T(8,128)(2,1)} %get-tuple-element.93), channel_id=1, source_target_pairs={{8,0},{16,8},{24,16},{9,1},{17,9},{25,17},{10,2},{18,10},{26,18},{... | collective-permute-start | bytes 1081352 | tf_op jit(solution)/shard_map/ppermute | solution.py:930
  93.1 10.2 %collective-permute-start.10 = (bf16[80,256]{1,0:T(8,128)(2,1)}, bf16[80,256]{1,0:T(8,128)(2,1)S(1)}, u32[]{:S(2)}, u32[]{:S(2)}) collective-permute-start(bf16[80,256]{1,0:T(8,128)(2,1)} %get-tuple-element.100), channel_id=1, source_target_pairs={{0,16},{8,24},{16,0},{24,8},{1,17},{9,25},{17,1},{25,9},{2,18},{10... | collective-permute-start | bytes 122888 | tf_op jit(solution)/shard_map/ppermute | solution.py:937
  97.4 36.1 %copy-start.4 = (bf16[240,1024]{1,0:T(8,128)(2,1)}, bf16[240,1024]{1,0:T(8,128)(2,1)S(1)}, u32[]{:S(2)}) copy-start(bf16[240,1024]{1,0:T(8,128)(2,1)S(1)} %collective-permute-done.8.refs_7_) | copy-start | bytes 1474564
  97.4 36.1 %copy-start.5 = (bf16[240,1024]{1,0:T(8,128)(2,1)}, bf16[240,1024]{1,0:T(8,128)(2,1)S(1)}, u32[]{:S(2)}) copy-start(bf16[240,1024]{1,0:T(8,128)(2,1)S(1)} %collective-permute-done.9.refs_8_) | copy-start | bytes 1474564
  103.3 0.8 copy-start.2
  104.1 0.8 copy-start.3
  107.4 26.0 %collective-permute-start.11 = (bf16[208,1024]{1,0:T(8,128)(2,1)S(1)}, bf16[208,1024]{1,0:T(8,128)(2,1)S(1)}, u32[]{:S(2)}, u32[]{:S(2)}) collective-permute-start(bf16[208,1024]{1,0:T(8,128)(2,1)S(1)} %copy-done.18), channel_id=1, source_target_pairs={{0,8},{8,16},{16,24},{1,9},{9,17},{17,25},{2,10},{10,18},{18,26},{... | collective-permute-start | bytes 1277960 | tf_op jit(solution)/shard_map/ppermute | solution.py:930
  108.7 24.7 %collective-permute-start.12 = (bf16[208,1024]{1,0:T(8,128)(2,1)S(1)}, bf16[208,1024]{1,0:T(8,128)(2,1)S(1)}, u32[]{:S(2)}, u32[]{:S(2)}) collective-permute-start(bf16[208,1024]{1,0:T(8,128)(2,1)S(1)} %copy-done.17), channel_id=1, source_target_pairs={{8,0},{16,8},{24,16},{9,1},{17,9},{25,17},{10,2},{18,10},{26,18},{... | collective-permute-start | bytes 1277960 | tf_op jit(solution)/shard_map/ppermute | solution.py:930
  110.0 10.0 %collective-permute-start.15 = (bf16[256,256]{1,0:T(8,128)(2,1)}, bf16[256,256]{1,0:T(8,128)(2,1)S(1)}, u32[]{:S(2)}, u32[]{:S(2)}) collective-permute-start(bf16[256,256]{1,0:T(8,128)(2,1)} %get-tuple-element.112), channel_id=1, source_target_pairs={{0,2},{1,3},{2,4},{3,5},{4,6},{5,7},{8,10},{9,11},{10,12},{11,13},... | collective-permute-start | bytes 393224 | tf_op jit(solution)/shard_map/ppermute | solution.py:930
  116.0 17.4 %collective-permute-start.13 = (bf16[448,256]{1,0:T(8,128)(2,1)}, bf16[448,256]{1,0:T(8,128)(2,1)S(1)}, u32[]{:S(2)}, u32[]{:S(2)}) collective-permute-start(bf16[448,256]{1,0:T(8,128)(2,1)} %get-tuple-element.110), channel_id=1, source_target_pairs={{0,1},{1,2},{2,3},{3,4},{4,5},{5,6},{6,7},{8,9},{9,10},{10,11},{11... | collective-permute-start | bytes 688136 | tf_op jit(solution)/shard_map/ppermute | solution.py:930
  118.0 15.3 %collective-permute-start.14 = (bf16[448,256]{1,0:T(8,128)(2,1)}, bf16[448,256]{1,0:T(8,128)(2,1)S(1)}, u32[]{:S(2)}, u32[]{:S(2)}) collective-permute-start(bf16[448,256]{1,0:T(8,128)(2,1)} %get-tuple-element.111), channel_id=1, source_target_pairs={{1,0},{2,1},{3,2},{4,3},{5,4},{6,5},{7,6},{9,8},{10,9},{11,10},{12... | collective-permute-start | bytes 688136 | tf_op jit(solution)/shard_map/ppermute | solution.py:930
  120.0 13.4 %copy-start.15 = (bf16[256,256]{1,0:T(8,128)(2,1)}, bf16[256,256]{1,0:T(8,128)(2,1)S(1)}, u32[]{:S(2)}) copy-start(bf16[256,256]{1,0:T(8,128)(2,1)S(1)} %collective-permute-done.15.refs_12_) | copy-start | bytes 393220
  120.0 13.4 %collective-permute-start.16 = (bf16[256,256]{1,0:T(8,128)(2,1)}, bf16[256,256]{1,0:T(8,128)(2,1)S(1)}, u32[]{:S(2)}, u32[]{:S(2)}) collective-permute-start(bf16[256,256]{1,0:T(8,128)(2,1)} %get-tuple-element.113), channel_id=1, source_target_pairs={{2,0},{3,1},{4,2},{5,3},{6,4},{7,5},{10,8},{11,9},{12,10},{13,11},... | collective-permute-start | bytes 393224 | tf_op jit(solution)/shard_map/ppermute | solution.py:930
  133.4 0.8 copy-start.11
  133.4 0.9 copy-start.6
  133.4 1.1 copy-start.7
  (4 other events, 2.8 us)
where the time goes:
time: 158 us; the launch traced here: 157 us
  Pallas kernels  81.6 us (52%)
  starting transfers between devices  45 us (28%)
  waiting for transfers between devices  25.3 us (16%)
  local copies, waits for them, and re-layouts  4.28 us (3%)
    pallas_call x8, Pallas kernels, call(): pl.pallas_call(kernel, out_shape=tuple(outs), in_specs=[SMEM] * smem + [V...  81.6 us
    ppermute x16, starting transfers between devices, both_ways(): return (lax.ppermute(to_high, axis, up), lax.ppermute(to_low, axis, down))  40.8 us
    ppermute x16, waiting for transfers between devices, both_ways(): return (lax.ppermute(to_high, axis, up), lax.ppermute(to_low, axis, down))  19.4 us
    ppermute x1, waiting for transfers between devices, two_away(): came = lax.ppermute(to_low, 'gz', [(i, (i + 2) % 4) for i in range(4)])  5.9 us
    unnamed x38, local copies, waits for them, and re-layouts  4.28 us
    ppermute x1, starting transfers between devices, two_away(): came = lax.ppermute(to_low, 'gz', [(i, (i + 2) % 4) for i in range(4)])  4.24 us
  transfers between devices with their start and end apart: 17, of which 6 were waited for; matrix products, arithmetic and copies ran while one was open for 0% of the time, Pallas kernels for 16%

commit v1 on v0

--- a/solution.py
+++ b/solution.py
@@ -621,7 +621,7 @@
 LOW_PACK = (4, (-2, 4, 2))
 
 
-def middle_kernel(nz, nx, c1, q_in, r2, cnl, cnh, mxl, mxh, f1, g1, v1, g2, z1l, z1h, z2l, z2h, q0, va, vv, rs, xp):
+def middle_kernel(nz, nx, c1, q_in, r2, cnl, cnh, vzl, vzh, mxl, mxh, f1, g1, v1, g2, z1l, z1h, z2l, z2h, q0, va, vv, rs, xp):
     iz, ix = lax.axis_index("gz"), lax.axis_index("xy")
     k = spread(1)
     base = 1.0 + 6.0 * k
@@ -670,9 +670,11 @@
         for ref in (z1l, z1h):
             ref[240:288, lanes(t)] = tile[0:6].reshape(48, 128).astype(BF16)
             ref[240:288, lanes(2 + t)] = tile[6:12].reshape(48, 128).astype(BF16)
-    for ref, corners in ((z1l, cnl), (z1h, cnh)):
+    for ref, corners, level0 in ((z1l, cnl, vzl), (z1h, cnh, vzh)):
         ref[288:320, :] = corners[:, 0:512]
         ref[320:352, :] = corners[:, 512:1024]
+        ref[352:560, :] = level0[:, 0:512]
+        ref[560:768, :] = level0[:, 512:1024]
     for ref, p in ((z1l, 2), (z1h, 18)):
         ref[0:144, :] = vv[p : p + 6].reshape(144, 512).astype(BF16)
         ref[144:240, :] = f1[p : p + 4].reshape(96, 512).astype(BF16)
@@ -685,7 +687,7 @@
 
 
 def back_kernel(
-    nz, nx, f_in, g1, v1, z1l, z1h, vzl, vzh, vxl_in, vxh_in, own2, n2l, n2h, m2l, m2h, q_own, v_in, g_in, s_in,
+    nz, nx, f_in, g1, v1, z1l, z1h, vxl_in, vxh_in, own2, n2l, n2h, m2l, m2h, q_own, v_in, g_in, s_in,
     out_hbm,
     f2, q2, h2, a2, b2, rs, xp, xpr, wa, w1, zsl, zsh, vb, ws,
     v2, gg, supply, fsl, fsh, out, f1, vxl, vxh, sems,
@@ -819,8 +821,9 @@
 
     for copy in level0:
         copy.wait()
-    zsl[...] = vzl[...].astype(F32)
-    zsh[...] = vzh[...].astype(F32)
+    for ref, message in ((zsl, z1l), (zsh, z1h)):
+        ref[:, 0:512] = message[352:560, :].astype(F32)
+        ref[:, 512:1024] = message[560:768, :].astype(F32)
     for ref, src, near in ((vxl, vxl_in, n2l), (vxh, vxh_in, n2h)):
         ref[...] = src[0:176, :]
         for n in range(4):
@@ -1034,25 +1037,23 @@
         (r2, zl, zh, v2, supply),
         in_hbm=2,
     )
-    pxl, pxh, vzl, vzh, c1 = lax.optimization_barrier((pxl, pxh, vzl, vzh, c1))
     pxl, pxh, mxl, mxh = lax.optimization_barrier((pxl, pxh, mxl, mxh))
     vxl, vxh = both_ways(pxl, pxh, "xy")
     f1, g1, v1, g2, z1l, z1h, z2l, z2h = call(
         lambda *refs: middle_kernel(nz, nx, *refs),
         [
             full(24, 24, 512), full(24, 24, 512), full(24, 24, 512), full(96, 256),
-            half(352, 512), half(352, 512), half(FAR, 256), half(FAR, 256),
+            half(768, 512), half(768, 512), half(FAR, 256), half(FAR, 256),
         ],
         [
             scratch((24, 24, 512), F32), scratch((24, 24, 512), F32), scratch((26, 24, 512), F32),
             scratch((4, 16, 128), F32), scratch((4, 12, 8, 128), F32),
         ],
         0,
-        (c1, q1, r2, cnl, cnh, mxl, mxh),
+        (c1, q1, r2, cnl, cnh, vzl, vzh, mxl, mxh),
     )
     z1l, z1h = both_ways(z1l, z1h, "gz")
     z2l, z2h = two_away(z2l, z2h)
-    g2, vxl, vxh = lax.optimization_barrier((g2, vxl, vxh))
     own2, q2, nl, nh, fl, fh = call(
         lambda *refs: source_window_kernel(nz, *refs),
         [full(32, 8, 256), full(32, 8, 256), half(448, 256), half(448, 256), half(256, 256), half(256, 256)],
@@ -1060,9 +1061,7 @@
         0,
         (g2, z1l, z1h, z2l, z2h, r2, zl, zh),
     )
-    vzl, vzh, nl, nh, fl, fh = lax.optimization_barrier((vzl, vzh, nl, nh, fl, fh))
     nl, nh = both_ways(nl, nh, "xy")
-    vzl, vzh = both_ways(vzl, vzh, "gz")
     fl, fh = both_ways(fl, fh, "xy", 2)
     window2 = scratch((32, 32, 256), F32)
     window1 = scratch((24, 24, 512), F32)
@@ -1091,7 +1090,7 @@
             pltpu.SemaphoreType.DMA((7,)),
         ],
         0,
-        (f1, g1, v1, z1l, z1h, vzl, vzh, vxl, vxh, own2, nl, nh, fl, fh, q2, v2, gg, supply),
+        (f1, g1, v1, z1l, z1h, vxl, vxh, own2, nl, nh, fl, fh, q2, v2, gg, supply),
         [ANY],
         in_hbm=3,
     )

time: 158 us -> 154 us (0.975)
  the two profiles are of different devices: /device:TPU:0 before, /device:TPU:22 now
where the time goes in v1:
time: 154 us; the launch traced here: 153 us
  Pallas kernels  82.3 us (53%)
  starting transfers between devices  40.5 us (26%)
  waiting for transfers between devices  24.8 us (16%)
  local copies, waits for them, and re-layouts  4.35 us (3%)
    pallas_call x8, Pallas kernels, call(): pl.pallas_call(kernel, out_shape=tuple(outs), in_specs=[SMEM] * smem + [V...  82.3 us
    ppermute x14, starting transfers between devices, both_ways(): return (lax.ppermute(to_high, axis, up), lax.ppermute(to_low, axis, down))  40.4 us
    ppermute x14, waiting for transfers between devices, both_ways(): return (lax.ppermute(to_high, axis, up), lax.ppermute(to_low, axis, down))  20.2 us
    ppermute x1, waiting for transfers between devices, two_away(): came = lax.ppermute(to_low, 'gz', [(i, (i + 2) % 4) for i in range(4)])  4.56 us
    unnamed x30, local copies, waits for them, and re-layouts  4.35 us
  transfers between devices with their start and end apart: 15, of which 6 were waited for; matrix products, arithmetic and copies ran while one was open for 0% of the time, Pallas kernels for 14%

profile of v1, /device:TPU:22, one launch (start us, length us, event | category | flops | bytes accessed | tf_op | source)
XLA Modules:
  0.0 153.0 jit_solution(5211535398498813527)
XLA Ops:
  0.6 7.4 %shard_map.68 = (bf16[272,384]{1,0:T(8,128)(2,1)}, f32[16,16,512]{2,1,0:T(8,128)}, f32[64,256]{1,0:T(8,128)}, bf16[592,384]{1,0:T(8,128)(2,1)}, bf16[592,384]{1,...) custom-call(s32[72]{0:T(128)} %refs_0_.1, s32[1,9]{1,0:T(1,128)} %refs_1_.1, ...), custom_call_target="tpu_custom_call" | custom-call | flops 135092560 | bytes 6754628 | tf_op jit(solution)/shard_map/pallas_call | solution.py:914
  8.0 1.9 %collective-permute-start = (bf16[592,384]{1,0:T(8,128)(2,1)}, bf16[592,384]{1,0:T(8,128)(2,1)S(1)}, u32[]{:S(2)}, u32[]{:S(2)}) collective-permute-start(bf16[592,384]{1,0:T(8,128)(2,1)} %get-tuple-element.49), channel_id=1, source_target_pairs={{0,8},{8,16},{16,24},{1,9},{9,17},{17,25},{2,10},{10,18},{18,26},{... | collective-permute-start | bytes 1363976 | tf_op jit(solution)/shard_map/ppermute | solution.py:933
  10.0 3.6 %collective-permute-start.1 = (bf16[592,384]{1,0:T(8,128)(2,1)}, bf16[592,384]{1,0:T(8,128)(2,1)S(1)}, u32[]{:S(2)}, u32[]{:S(2)}) collective-permute-start(bf16[592,384]{1,0:T(8,128)(2,1)} %get-tuple-element.50), channel_id=1, source_target_pairs={{8,0},{16,8},{24,16},{9,1},{17,9},{25,17},{10,2},{18,10},{26,18},{... | collective-permute-start | bytes 1363976 | tf_op jit(solution)/shard_map/ppermute | solution.py:933
  13.6 4.4 %collective-permute-done.zl.refs_1_.refs_2_.refs_6_ = bf16[592,384]{1,0:T(8,128)(2,1)S(1)} collective-permute-done((bf16[592,384]{1,0:T(8,128)(2,1)}, bf16[592,384]{1,0:T(8,128)(2,1)S(1)}, u32[]{:S(2)}, u32[]{:S(2)}) %collective-permute-start) | collective-permute-done | bytes 454688 | tf_op jit(solution)/shard_map/ppermute | solution.py:933
  18.0 1.9 %collective-permute-done.1.zh.refs_2_.refs_3_.refs_7_ = bf16[592,384]{1,0:T(8,128)(2,1)S(1)} collective-permute-done((bf16[592,384]{1,0:T(8,128)(2,1)}, bf16[592,384]{1,0:T(8,128)(2,1)S(1)}, u32[]{:S(2)}, u32[]{:S(2)}) %collective-permute-start.1) | collective-permute-done | bytes 454688 | tf_op jit(solution)/shard_map/ppermute | solution.py:933
  19.9 0.8 copy-done.1
  20.7 2.6 %shard_map.69 = (f32[24,16,512]{2,1,0:T(8,128)}, bf16[464,384]{1,0:T(8,128)(2,1)}, bf16[464,384]{1,0:T(8,128)(2,1)}) custom-call(bf16[272,384]{1,0:T(8,128)(2,1)} %get-tuple-element.45.own.refs_0_, f32[16,16,512]{2,1,0:T(8,128)} %get-tuple-element.46.r1, bf16[64,1024]{1,0:T(8,128)(2,1)} %get-tuple-element.47.uxl, bf16[64,1024]{1,0:T(8,128)(2,1)} %get-tuple-element.48.uxh, ...), custom_call_target="tpu_custom_call" | custom-call | flops 68075520 | bytes 3403776 | tf_op jit(solution)/shard_map/pallas_call | solution.py:914
  23.3 3.4 %collective-permute-start.2 = (bf16[464,384]{1,0:T(8,128)(2,1)}, bf16[464,384]{1,0:T(8,128)(2,1)S(1)}, u32[]{:S(2)}, u32[]{:S(2)}) collective-permute-start(bf16[464,384]{1,0:T(8,128)(2,1)} %get-tuple-element.51), channel_id=1, source_target_pairs={{0,1},{1,2},{2,3},{3,4},{4,5},{5,6},{6,7},{8,9},{9,10},{10,11},{11... | collective-permute-start | bytes 1069064 | tf_op jit(solution)/shard_map/ppermute | solution.py:933
  26.8 2.4 %collective-permute-start.3 = (bf16[464,384]{1,0:T(8,128)(2,1)}, bf16[464,384]{1,0:T(8,128)(2,1)S(1)}, u32[]{:S(2)}, u32[]{:S(2)}) collective-permute-start(bf16[464,384]{1,0:T(8,128)(2,1)} %get-tuple-element.52), channel_id=1, source_target_pairs={{1,0},{2,1},{3,2},{4,3},{5,4},{6,5},{7,6},{9,8},{10,9},{11,10},{12... | collective-permute-start | bytes 1069064 | tf_op jit(solution)/shard_map/ppermute | solution.py:933
  29.2 12.2 %shard_map.70 = (f32[32,32,1024]{2,1,0:T(8,128)}, f32[36,32,1024]{2,1,0:T(8,128)}, f32[34,32,1024]{2,1,0:T(8,128)}, f32[32,8,1024]{2,1,0:T(8,128)}) custom-call(bf16[272,384]{1,0:T(8,128)(2,1)} %get-tuple-element.45.own.refs_0_, bf16[592,384]{1,0:T(8,128)(2,1)} %copy-done, bf16[592,384]{1,0:T(8,128)(2,1)} %copy-done.1, f32[32,32,1024]{2,1,0:T(8,128)} %refs_3_.3, ...), custom_call_target="tpu_custom_call" | custom-call | flops 478494720 | bytes 23924736 | tf_op jit(solution)/shard_map/pallas_call | solution.py:914
  41.5 0.8 copy-done.6
  42.3 20.8 %shard_map.71 = (f32[20,24,512]{2,1,0:T(8,128)}, bf16[224,512]{1,0:T(8,128)(2,1)}, bf16[224,512]{1,0:T(8,128)(2,1)}, f32[36,40,1024]{2,1,0:T(8,128)}, f32[36,40,1024]{2,1,0:T(8,128)}, /*index=5*/f32[32,32,1024]{2,1,0:T(8,128)}) custom-call(bf16[464,384]{1,0:T(8,128)(2,1)} %copy-done.6, bf16[464,384]{1,0:T(8,128)(2,1)} %copy-done.7, ...), custom_call_target="tpu_custom_call" | custom-call | flops 769064960 | bytes 38453248 | tf_op jit(solution)/shard_map/pallas_call | solution.py:914
  63.1 4.4 %collective-permute-start.4 = (bf16[224,512]{1,0:T(8,128)(2,1)}, bf16[224,512]{1,0:T(8,128)(2,1)S(1)}, u32[]{:S(2)}, u32[]{:S(2)}) collective-permute-start(bf16[224,512]{1,0:T(8,128)(2,1)} %get-tuple-element.68), channel_id=1, source_target_pairs={{0,1},{1,2},{2,3},{3,4},{4,5},{5,6},{6,7},{8,9},{9,10},{10,11},{11... | collective-permute-start | bytes 688136 | tf_op jit(solution)/shard_map/ppermute | solution.py:933
  67.5 1.9 %collective-permute-start.5 = (bf16[224,512]{1,0:T(8,128)(2,1)}, bf16[224,512]{1,0:T(8,128)(2,1)S(1)}, u32[]{:S(2)}, u32[]{:S(2)}) collective-permute-start(bf16[224,512]{1,0:T(8,128)(2,1)} %get-tuple-element.69), channel_id=1, source_target_pairs={{1,0},{2,1},{3,2},{4,3},{5,4},{6,5},{7,6},{9,8},{10,9},{11,10},{12... | collective-permute-start | bytes 688136 | tf_op jit(solution)/shard_map/ppermute | solution.py:933
  69.4 6.1 %shard_map.72 = (bf16[208,1024]{1,0:T(8,128)(2,1)}, bf16[208,1024]{1,0:T(8,128)(2,1)}, bf16[240,1024]{1,0:T(8,128)(2,1)}, bf16[240,1024]{1,0:T(8,128)(2,1)}, bf1...) custom-call(f32[64,256]{1,0:T(8,128)} %get-tuple-element.60.r2.refs_2_.refs_5_, bf16[592,384]{1,0:T(8,128)(2,1)} %copy-done, ...), custom_call_target="tpu_custom_call" | custom-call | flops 260669440 | bytes 13033472 | tf_op jit(solution)/shard_map/pallas_call | solution.py:914
  75.5 1.0 collective-permute-done.5.refs_8_
  76.5 0.7 copy-done.11
  77.2 7.8 %shard_map.73 = (f32[24,24,512]{2,1,0:T(8,128)}, f32[24,24,512]{2,1,0:T(8,128)}, f32[24,24,512]{2,1,0:T(8,128)}, f32[96,256]{1,0:T(8,128)}, bf16[768,512]{1,0:T(...) custom-call(f32[20,24,512]{2,1,0:T(8,128)} %get-tuple-element.59.refs_0_, ...), custom_call_target="tpu_custom_call" | custom-call | flops 171376640 | bytes 8568832 | tf_op jit(solution)/shard_map/pallas_call | solution.py:914
  85.0 1.9 %collective-permute-start.6 = (bf16[768,512]{1,0:T(8,128)(2,1)}, bf16[768,512]{1,0:T(8,128)(2,1)S(1)}, u32[]{:S(2)}, u32[]{:S(2)}) collective-permute-start(bf16[768,512]{1,0:T(8,128)(2,1)} %get-tuple-element.75), channel_id=1, source_target_pairs={{0,8},{8,16},{16,24},{1,9},{9,17},{17,25},{2,10},{10,18},{18,26},{... | collective-permute-start | bytes 2359304 | tf_op jit(solution)/shard_map/ppermute | solution.py:933
  86.9 3.6 %collective-permute-start.7 = (bf16[768,512]{1,0:T(8,128)(2,1)}, bf16[768,512]{1,0:T(8,128)(2,1)S(1)}, u32[]{:S(2)}, u32[]{:S(2)}) collective-permute-start(bf16[768,512]{1,0:T(8,128)(2,1)} %get-tuple-element.76), channel_id=1, source_target_pairs={{8,0},{16,8},{24,16},{9,1},{17,9},{25,17},{10,2},{18,10},{26,18},{... | collective-permute-start | bytes 2359304 | tf_op jit(solution)/shard_map/ppermute | solution.py:933
  90.6 3.9 %collective-permute-start.8 = (bf16[240,1024]{1,0:T(8,128)(2,1)}, bf16[240,1024]{1,0:T(8,128)(2,1)S(1)}, u32[]{:S(2)}, u32[]{:S(2)}) collective-permute-start(bf16[240,1024]{1,0:T(8,128)(2,1)} %get-tuple-element.77), channel_id=1, source_target_pairs={{0,1},{1,2},{2,3},{3,4},{4,5},{5,6},{6,7},{8,9},{9,10},{10,11},{11... | collective-permute-start | bytes 1474568 | tf_op jit(solution)/shard_map/ppermute | solution.py:933
  94.5 2.1 %collective-permute-start.9 = (bf16[240,1024]{1,0:T(8,128)(2,1)}, bf16[240,1024]{1,0:T(8,128)(2,1)S(1)}, u32[]{:S(2)}, u32[]{:S(2)}) collective-permute-start(bf16[240,1024]{1,0:T(8,128)(2,1)} %get-tuple-element.78), channel_id=1, source_target_pairs={{1,0},{2,1},{3,2},{4,3},{5,4},{6,5},{7,6},{9,8},{10,9},{11,10},{12... | collective-permute-start | bytes 1474568 | tf_op jit(solution)/shard_map/ppermute | solution.py:933
  96.7 4.6 %collective-permute-done.10.refs_3_.refs_4_ = bf16[80,256]{1,0:T(8,128)(2,1)S(1)} collective-permute-done((bf16[80,256]{1,0:T(8,128)(2,1)}, bf16[80,256]{1,0:T(8,128)(2,1)S(1)}, u32[]{:S(2)}, u32[]{:S(2)}) %collective-permute-start.10) | collective-permute-done | bytes 40992 | tf_op jit(solution)/shard_map/ppermute | solution.py:940
  102.4 2.7 %shard_map.74 = (f32[32,8,256]{2,1,0:T(8,128)}, f32[32,8,256]{2,1,0:T(8,128)}, bf16[448,256]{1,0:T(8,128)(2,1)}, bf16[448,256]{1,0:T(8,128)(2,1)}, bf16[256,256]{1,0:T(8,128)(2,1)}, /*index=5*/bf16[256,256]{1,0:T(8,128)(2,1)}) custom-call(f32[96,256]{1,0:T(8,128)} %get-tuple-element.79.refs_0_, bf16[768,512]{1,0:T(8,128)(2,1)} %copy-done.2, ...), custom_call_target="tpu_custom_call" | custom-call | flops 79462400 | bytes 3973120 | tf_op jit(solution)/shard_map/pallas_call | solution.py:914
  105.1 4.4 %collective-permute-start.11 = (bf16[448,256]{1,0:T(8,128)(2,1)}, bf16[448,256]{1,0:T(8,128)(2,1)S(1)}, u32[]{:S(2)}, u32[]{:S(2)}) collective-permute-start(bf16[448,256]{1,0:T(8,128)(2,1)} %get-tuple-element.82), channel_id=1, source_target_pairs={{0,1},{1,2},{2,3},{3,4},{4,5},{5,6},{6,7},{8,9},{9,10},{10,11},{11... | collective-permute-start | bytes 688136 | tf_op jit(solution)/shard_map/ppermute | solution.py:933
  109.6 1.9 %collective-permute-start.12 = (bf16[448,256]{1,0:T(8,128)(2,1)}, bf16[448,256]{1,0:T(8,128)(2,1)S(1)}, u32[]{:S(2)}, u32[]{:S(2)}) collective-permute-start(bf16[448,256]{1,0:T(8,128)(2,1)} %get-tuple-element.83), channel_id=1, source_target_pairs={{1,0},{2,1},{3,2},{4,3},{5,4},{6,5},{7,6},{9,8},{10,9},{11,10},{12... | collective-permute-start | bytes 688136 | tf_op jit(solution)/shard_map/ppermute | solution.py:933
  111.5 2.5 %collective-permute-start.13 = (bf16[256,256]{1,0:T(8,128)(2,1)}, bf16[256,256]{1,0:T(8,128)(2,1)S(1)}, u32[]{:S(2)}, u32[]{:S(2)}) collective-permute-start(bf16[256,256]{1,0:T(8,128)(2,1)} %get-tuple-element.84), channel_id=1, source_target_pairs={{0,2},{1,3},{2,4},{3,5},{4,6},{5,7},{8,10},{9,11},{10,12},{11,13},... | collective-permute-start | bytes 393224 | tf_op jit(solution)/shard_map/ppermute | solution.py:933
  114.0 8.3 %collective-permute-done.8.refs_5_ = bf16[240,1024]{1,0:T(8,128)(2,1)S(1)} collective-permute-done((bf16[240,1024]{1,0:T(8,128)(2,1)}, bf16[240,1024]{1,0:T(8,128)(2,1)S(1)}, u32[]{:S(2)}, u32[]{:S(2)}) %collective-permute-start.8) | collective-permute-done | bytes 491552 | tf_op jit(solution)/shard_map/ppermute | solution.py:933
  122.3 2.3 %collective-permute-start.14 = (bf16[256,256]{1,0:T(8,128)(2,1)}, bf16[256,256]{1,0:T(8,128)(2,1)S(1)}, u32[]{:S(2)}, u32[]{:S(2)}) collective-permute-start(bf16[256,256]{1,0:T(8,128)(2,1)} %get-tuple-element.85), channel_id=1, source_target_pairs={{2,0},{3,1},{4,2},{5,3},{6,4},{7,5},{10,8},{11,9},{12,10},{13,11},... | collective-permute-start | bytes 393224 | tf_op jit(solution)/shard_map/ppermute | solution.py:933
  124.7 4.7 %collective-permute-done.14.refs_11_ = bf16[256,256]{1,0:T(8,128)(2,1)S(1)} collective-permute-done((bf16[256,256]{1,0:T(8,128)(2,1)}, bf16[256,256]{1,0:T(8,128)(2,1)S(1)}, u32[]{:S(2)}, u32[]{:S(2)}) %collective-permute-start.14) | collective-permute-done | bytes 131104 | tf_op jit(solution)/shard_map/ppermute | solution.py:933
  129.4 0.6 copy-done.14
  130.2 22.7 %shard_map.75 = f32[32,32,1024]{2,1,0:T(8,128)} custom-call(f32[24,24,512]{2,1,0:T(8,128)} %get-tuple-element.72.refs_0_, f32[24,24,512]{2,1,0:T(8,128)} %get-tuple-element.73.refs_1_, f32[24,24,512]{2,1,0:T(8,128)} %get-tuple-element.74.refs_2_, bf16[768,512]{1,0:T(8,128)(2,1)} %copy-done.2, bf16[768,512]{1,0:T(8,128)(2,1)} %copy-done.3, ...), custom_call_target="tpu_custom_call" | custom-call | flops 550502400 | bytes 27525120 | tf_op jit(solution)/shard_map/pallas_call | solution.py:914
  (36 shorter events, 1.6 us)
Async XLA Ops:
  8.0 10.0 %collective-permute-start = (bf16[592,384]{1,0:T(8,128)(2,1)}, bf16[592,384]{1,0:T(8,128)(2,1)S(1)}, u32[]{:S(2)}, u32[]{:S(2)}) collective-permute-start(bf16[592,384]{1,0:T(8,128)(2,1)} %get-tuple-element.49), channel_id=1, source_target_pairs={{0,8},{8,16},{16,24},{1,9},{9,17},{17,25},{2,10},{10,18},{18,26},{... | collective-permute-start | bytes 1363976 | tf_op jit(solution)/shard_map/ppermute | solution.py:933
  10.0 9.9 %collective-permute-start.1 = (bf16[592,384]{1,0:T(8,128)(2,1)}, bf16[592,384]{1,0:T(8,128)(2,1)S(1)}, u32[]{:S(2)}, u32[]{:S(2)}) collective-permute-start(bf16[592,384]{1,0:T(8,128)(2,1)} %get-tuple-element.50), channel_id=1, source_target_pairs={{8,0},{16,8},{24,16},{9,1},{17,9},{25,17},{10,2},{18,10},{26,18},{... | collective-permute-start | bytes 1363976 | tf_op jit(solution)/shard_map/ppermute | solution.py:933
  18.0 1.9 %copy-start = (bf16[592,384]{1,0:T(8,128)(2,1)}, bf16[592,384]{1,0:T(8,128)(2,1)S(1)}, u32[]{:S(2)}) copy-start(bf16[592,384]{1,0:T(8,128)(2,1)S(1)} %collective-permute-done.zl.refs_1_.refs_2_.refs_6_) | copy-start | bytes 1363972
  19.9 0.8 copy-start.1
  23.3 18.1 %collective-permute-start.2 = (bf16[464,384]{1,0:T(8,128)(2,1)}, bf16[464,384]{1,0:T(8,128)(2,1)S(1)}, u32[]{:S(2)}, u32[]{:S(2)}) collective-permute-start(bf16[464,384]{1,0:T(8,128)(2,1)} %get-tuple-element.51), channel_id=1, source_target_pairs={{0,1},{1,2},{2,3},{3,4},{4,5},{5,6},{6,7},{8,9},{9,10},{10,11},{11... | collective-permute-start | bytes 1069064 | tf_op jit(solution)/shard_map/ppermute | solution.py:933
  26.8 14.6 %collective-permute-start.3 = (bf16[464,384]{1,0:T(8,128)(2,1)}, bf16[464,384]{1,0:T(8,128)(2,1)S(1)}, u32[]{:S(2)}, u32[]{:S(2)}) collective-permute-start(bf16[464,384]{1,0:T(8,128)(2,1)} %get-tuple-element.52), channel_id=1, source_target_pairs={{1,0},{2,1},{3,2},{4,3},{5,4},{6,5},{7,6},{9,8},{10,9},{11,10},{12... | collective-permute-start | bytes 1069064 | tf_op jit(solution)/shard_map/ppermute | solution.py:933
  41.4 0.8 copy-start.6
  41.4 0.9 copy-start.7
  63.1 12.4 %collective-permute-start.4 = (bf16[224,512]{1,0:T(8,128)(2,1)}, bf16[224,512]{1,0:T(8,128)(2,1)S(1)}, u32[]{:S(2)}, u32[]{:S(2)}) collective-permute-start(bf16[224,512]{1,0:T(8,128)(2,1)} %get-tuple-element.68), channel_id=1, source_target_pairs={{0,1},{1,2},{2,3},{3,4},{4,5},{5,6},{6,7},{8,9},{9,10},{10,11},{11... | collective-permute-start | bytes 688136 | tf_op jit(solution)/shard_map/ppermute | solution.py:933
  67.5 9.0 %collective-permute-start.5 = (bf16[224,512]{1,0:T(8,128)(2,1)}, bf16[224,512]{1,0:T(8,128)(2,1)S(1)}, u32[]{:S(2)}, u32[]{:S(2)}) collective-permute-start(bf16[224,512]{1,0:T(8,128)(2,1)} %get-tuple-element.69), channel_id=1, source_target_pairs={{1,0},{2,1},{3,2},{4,3},{5,4},{6,5},{7,6},{9,8},{10,9},{11,10},{12... | collective-permute-start | bytes 688136 | tf_op jit(solution)/shard_map/ppermute | solution.py:933
  75.5 1.0 copy-start.10
  76.5 0.7 copy-start.11
  85.0 16.3 %collective-permute-start.6 = (bf16[768,512]{1,0:T(8,128)(2,1)}, bf16[768,512]{1,0:T(8,128)(2,1)S(1)}, u32[]{:S(2)}, u32[]{:S(2)}) collective-permute-start(bf16[768,512]{1,0:T(8,128)(2,1)} %get-tuple-element.75), channel_id=1, source_target_pairs={{0,8},{8,16},{16,24},{1,9},{9,17},{17,25},{2,10},{10,18},{18,26},{... | collective-permute-start | bytes 2359304 | tf_op jit(solution)/shard_map/ppermute | solution.py:933
  86.9 14.3 %collective-permute-start.7 = (bf16[768,512]{1,0:T(8,128)(2,1)}, bf16[768,512]{1,0:T(8,128)(2,1)S(1)}, u32[]{:S(2)}, u32[]{:S(2)}) collective-permute-start(bf16[768,512]{1,0:T(8,128)(2,1)} %get-tuple-element.76), channel_id=1, source_target_pairs={{8,0},{16,8},{24,16},{9,1},{17,9},{25,17},{10,2},{18,10},{26,18},{... | collective-permute-start | bytes 2359304 | tf_op jit(solution)/shard_map/ppermute | solution.py:933
  90.6 31.7 %collective-permute-start.8 = (bf16[240,1024]{1,0:T(8,128)(2,1)}, bf16[240,1024]{1,0:T(8,128)(2,1)S(1)}, u32[]{:S(2)}, u32[]{:S(2)}) collective-permute-start(bf16[240,1024]{1,0:T(8,128)(2,1)} %get-tuple-element.77), channel_id=1, source_target_pairs={{0,1},{1,2},{2,3},{3,4},{4,5},{5,6},{6,7},{8,9},{9,10},{10,11},{11... | collective-permute-start | bytes 1474568 | tf_op jit(solution)/shard_map/ppermute | solution.py:933
  94.5 30.2 %collective-permute-start.9 = (bf16[240,1024]{1,0:T(8,128)(2,1)}, bf16[240,1024]{1,0:T(8,128)(2,1)S(1)}, u32[]{:S(2)}, u32[]{:S(2)}) collective-permute-start(bf16[240,1024]{1,0:T(8,128)(2,1)} %get-tuple-element.78), channel_id=1, source_target_pairs={{1,0},{2,1},{3,2},{4,3},{5,4},{6,5},{7,6},{9,8},{10,9},{11,10},{12... | collective-permute-start | bytes 1474568 | tf_op jit(solution)/shard_map/ppermute | solution.py:933
  96.6 4.6 %collective-permute-start.10 = (bf16[80,256]{1,0:T(8,128)(2,1)}, bf16[80,256]{1,0:T(8,128)(2,1)S(1)}, u32[]{:S(2)}, u32[]{:S(2)}) collective-permute-start(bf16[80,256]{1,0:T(8,128)(2,1)} %get-tuple-element.80), channel_id=1, source_target_pairs={{0,16},{8,24},{16,0},{24,8},{1,17},{9,25},{17,1},{25,9},{2,18},{10... | collective-permute-start | bytes 122888 | tf_op jit(solution)/shard_map/ppermute | solution.py:940
  101.3 0.6 copy-start.12
  101.3 0.9 copy-start.2
  101.3 1.1 copy-start.3
  105.1 24.2 %collective-permute-start.11 = (bf16[448,256]{1,0:T(8,128)(2,1)}, bf16[448,256]{1,0:T(8,128)(2,1)S(1)}, u32[]{:S(2)}, u32[]{:S(2)}) collective-permute-start(bf16[448,256]{1,0:T(8,128)(2,1)} %get-tuple-element.82), channel_id=1, source_target_pairs={{0,1},{1,2},{2,3},{3,4},{4,5},{5,6},{6,7},{8,9},{9,10},{10,11},{11... | collective-permute-start | bytes 688136 | tf_op jit(solution)/shard_map/ppermute | solution.py:933
  109.6 19.8 %collective-permute-start.12 = (bf16[448,256]{1,0:T(8,128)(2,1)}, bf16[448,256]{1,0:T(8,128)(2,1)S(1)}, u32[]{:S(2)}, u32[]{:S(2)}) collective-permute-start(bf16[448,256]{1,0:T(8,128)(2,1)} %get-tuple-element.83), channel_id=1, source_target_pairs={{1,0},{2,1},{3,2},{4,3},{5,4},{6,5},{7,6},{9,8},{10,9},{11,10},{12... | collective-permute-start | bytes 688136 | tf_op jit(solution)/shard_map/ppermute | solution.py:933
  111.5 13.2 %collective-permute-start.13 = (bf16[256,256]{1,0:T(8,128)(2,1)}, bf16[256,256]{1,0:T(8,128)(2,1)S(1)}, u32[]{:S(2)}, u32[]{:S(2)}) collective-permute-start(bf16[256,256]{1,0:T(8,128)(2,1)} %get-tuple-element.84), channel_id=1, source_target_pairs={{0,2},{1,3},{2,4},{3,5},{4,6},{5,7},{8,10},{9,11},{10,12},{11,13},... | collective-permute-start | bytes 393224 | tf_op jit(solution)/shard_map/ppermute | solution.py:933
  122.3 7.1 %copy-start.4 = (bf16[240,1024]{1,0:T(8,128)(2,1)}, bf16[240,1024]{1,0:T(8,128)(2,1)S(1)}, u32[]{:S(2)}) copy-start(bf16[240,1024]{1,0:T(8,128)(2,1)S(1)} %collective-permute-done.8.refs_5_) | copy-start | bytes 1474564
  122.3 7.1 %collective-permute-start.14 = (bf16[256,256]{1,0:T(8,128)(2,1)}, bf16[256,256]{1,0:T(8,128)(2,1)S(1)}, u32[]{:S(2)}, u32[]{:S(2)}) collective-permute-start(bf16[256,256]{1,0:T(8,128)(2,1)} %get-tuple-element.85), channel_id=1, source_target_pairs={{2,0},{3,1},{4,2},{5,3},{6,4},{7,5},{10,8},{11,9},{12,10},{13,11},... | collective-permute-start | bytes 393224 | tf_op jit(solution)/shard_map/ppermute | solution.py:933
  124.7 4.7 %copy-start.5 = (bf16[240,1024]{1,0:T(8,128)(2,1)}, bf16[240,1024]{1,0:T(8,128)(2,1)S(1)}, u32[]{:S(2)}) copy-start(bf16[240,1024]{1,0:T(8,128)(2,1)S(1)} %collective-permute-done.9.refs_6_) | copy-start | bytes 1474564
  124.7 4.7 %copy-start.13 = (bf16[256,256]{1,0:T(8,128)(2,1)}, bf16[256,256]{1,0:T(8,128)(2,1)S(1)}, u32[]{:S(2)}) copy-start(bf16[256,256]{1,0:T(8,128)(2,1)S(1)} %collective-permute-done.13.refs_10_) | copy-start | bytes 393220
  129.4 0.6 copy-start.14
  129.4 0.7 copy-start.8
  129.4 0.8 copy-start.9

commit v2 on v1

--- a/solution.py
+++ b/solution.py
@@ -97,12 +97,18 @@
 
 
 BLOCK = 272
-X_ROWS = BLOCK + 3 * 64
+X_ROWS = BLOCK + 3 * 64 + 2 * 64
 Z_ROWS = BLOCK + 5 * 64
 
 
 def uptake_part(t):
     return slice(BLOCK + 64 * (t // 3), BLOCK + 64 * (t // 3) + 64), lanes(t % 3)
+
+
+def rates2_part(n, t):
+    k = 3 * t + n
+    first = BLOCK + 3 * 64 + 64 * (k % 2)
+    return slice(first, first + 64), lanes(k // 2)
 
 
 def transposed_bricks(bricks_x, ids, counts, bricks, xs, targets):
@@ -221,7 +227,7 @@
     return jnp.stack([even, odd], axis=1).reshape(-1, 8, width)
 
 
-def first_x_kernel(own, r1, uxl, uxh, zl, zh, q1, xl, xh):
+def first_x_kernel(own, r1, r2, uxl, uxh, zl, zh, q1, xl, xh):
     q1[4:20] = r1[...]
     for ref, planes in ((zl, slice(0, 4)), (zh, slice(20, 24))):
         for t in range(4):
@@ -229,6 +235,10 @@
     for ref, d in ((xl, 0), (xh, 2)):
         for n, src in enumerate((own, zl, zh)):
             ref[0:BLOCK, lanes(n)] = src[0:BLOCK, lanes(d)]
+        for t in range(2):
+            ref[rates2_part(0, t)] = zl[uptake_part(12 + t)]
+            ref[rates2_part(1, t)] = r2[:, lanes(t)].astype(BF16)
+            ref[rates2_part(2, t)] = zh[uptake_part(12 + t)]
     sub = iota((8, 128), 0)
     lows, highs = [], []
     for t in range(8):
@@ -517,7 +527,7 @@
     s_copy.wait()
 
 
-def edges_kernel(r2, zl, zh, v_in, s_in, vzl, vzh, pxl, pxh, cnl, cnh, vx, vz, sx, sz, sems):
+def edges_kernel(v_in, s_in, vzl, vzh, pxl, pxh, cnl, cnh, vx, vz, sx, sz, sems):
     copies = [
         (v_in.at[:, 0:8, :], vx.at[:, 0:8, :]),
         (v_in.at[:, 24:40, :], vx.at[:, 8:24, :]),
@@ -532,12 +542,6 @@
     for copy in copies:
         copy.start()
     sub8 = iota((8, 1024), 0)
-    for ref in (pxl, pxh):
-        for t in range(2):
-            ref[176:240, lanes(t)] = zl[uptake_part(12 + t)]
-            ref[176:240, lanes(2 + t)] = r2[:, lanes(t)].astype(BF16)
-            ref[176:240, lanes(4 + t)] = zh[uptake_part(12 + t)]
-        ref[176:240, 768:1024] = jnp.zeros((64, 256), BF16)
     for copy in copies:
         copy.wait()
 
@@ -687,7 +691,7 @@
 
 
 def back_kernel(
-    nz, nx, f_in, g1, v1, z1l, z1h, vxl_in, vxh_in, own2, n2l, n2h, m2l, m2h, q_own, v_in, g_in, s_in,
+    nz, nx, f_in, g1, v1, z1l, z1h, xl, xh, vxl_in, vxh_in, own2, n2l, n2h, m2l, m2h, q_own, v_in, g_in, s_in,
     out_hbm,
     f2, q2, h2, a2, b2, rs, xp, xpr, wa, w1, zsl, zsh, vb, ws,
     v2, gg, supply, fsl, fsh, out, f1, vxl, vxh, sems,
@@ -713,9 +717,11 @@
     f2[:, 24:32, :] = n2l[0:256, :].astype(F32).reshape(32, 8, 256)
     q2[:, 0:8, :] = q_own[...]
     q2[:, 16:24, :] = far_tile(m2l[128:256, :].astype(F32), m2h[128:256, :].astype(F32))
-    for ref, rows in ((vxh_in, slice(8, 16)), (vxl_in, slice(24, 32))):
+    for ref, rows in ((xh, slice(8, 16)), (xl, slice(24, 32))):
         for n in range(3):
-            q2[8 * n + 4 : 8 * n + 12, rows, :] = ref[176:240, n * 256 : n * 256 + 256].astype(F32).reshape(8, 8, 256)
+            for t in range(2):
+                part = ref[rates2_part(n, t)].astype(F32).reshape(8, 8, 128)
+                q2[8 * n + 4 : 8 * n + 12, rows, lanes(t)] = part
     for ref, rows in ((n2h, slice(8, 16)), (n2l, slice(24, 32))):
         outer = ref[256:320, :].astype(F32).reshape(8, 8, 256)
         q2[0:4, rows, :] = outer[0:4]
@@ -825,7 +831,7 @@
         ref[:, 0:512] = message[352:560, :].astype(F32)
         ref[:, 512:1024] = message[560:768, :].astype(F32)
     for ref, src, near in ((vxl, vxl_in, n2l), (vxh, vxh_in, n2h)):
-        ref[...] = src[0:176, :]
+        ref[...] = src[...]
         for n in range(4):
             cols = slice(256 * n, 256 * n + 256)
             for i, rows in enumerate((slice(0, 16), slice(128, 144))):
@@ -968,7 +974,7 @@
         [full(24, 16, 512), half(X_ROWS, 384), half(X_ROWS, 384)],
         [],
         0,
-        (own, r1, uxl, uxh, zl, zh),
+        (own, r1, r2, uxl, uxh, zl, zh),
     )
     s0, g0, v1, edge = call(
         lambda *refs: own_kernel(nz, *refs),
@@ -1027,14 +1033,14 @@
     vzl, vzh, pxl, pxh, cnl, cnh = call(
         edges_kernel,
         [
-            half(208, 1024), half(208, 1024), half(240, 1024), half(240, 1024), half(32, 1024), half(32, 1024),
+            half(208, 1024), half(208, 1024), half(176, 1024), half(176, 1024), half(32, 1024), half(32, 1024),
         ],
         [
             scratch((36, 24, 1024), F32), scratch((2, 4, 40, 1024), F32), scratch((C, 16, 1024), F32),
             scratch((2, C, 1024), F32), pltpu.SemaphoreType.DMA((8,)),
         ],
         0,
-        (r2, zl, zh, v2, supply),
+        (v2, supply),
         in_hbm=2,
     )
     pxl, pxh, mxl, mxh = lax.optimization_barrier((pxl, pxh, mxl, mxh))
@@ -1090,7 +1096,7 @@
             pltpu.SemaphoreType.DMA((7,)),
         ],
         0,
-        (f1, g1, v1, z1l, z1h, vxl, vxh, own2, nl, nh, fl, fh, q2, v2, gg, supply),
+        (f1, g1, v1, z1l, z1h, xl, xh, vxl, vxh, own2, nl, nh, fl, fh, q2, v2, gg, supply),
         [ANY],
         in_hbm=3,
     )

time: 154 us -> 154 us (level)
  the two profiles are of different devices: /device:TPU:22 before, /device:TPU:0 now
where the time goes in v2:
time: 154 us; the launch traced here: 153 us
  Pallas kernels  81.5 us (53%)
  starting transfers between devices  39.9 us (26%)
  waiting for transfers between devices  26.3 us (17%)
  local copies, waits for them, and re-layouts  4.39 us (3%)
    pallas_call x8, Pallas kernels, call(): pl.pallas_call(kernel, out_shape=tuple(outs), in_specs=[SMEM] * smem + [V...  81.5 us
    ppermute x14, starting transfers between devices, both_ways(): return (lax.ppermute(to_high, axis, up), lax.ppermute(to_low, axis, down))  37.7 us
    ppermute x14, waiting for transfers between devices, both_ways(): return (lax.ppermute(to_high, axis, up), lax.ppermute(to_low, axis, down))  21.2 us
    ppermute x1, waiting for transfers between devices, two_away(): came = lax.ppermute(to_low, 'gz', [(i, (i + 2) % 4) for i in range(4)])  5.11 us
    unnamed x30, local copies, waits for them, and re-layouts  4.39 us
  transfers between devices with their start and end apart: 15, of which 7 were waited for; matrix products, arithmetic and copies ran while one was open for 0% of the time, Pallas kernels for 13%

profile of v2, /device:TPU:0, one launch (start us, length us, event | category | flops | bytes accessed | tf_op | source)
XLA Modules:
  0.0 153.2 jit_solution(1043994614232284777)
XLA Ops:
  0.6 7.4 %shard_map.68 = (bf16[272,384]{1,0:T(8,128)(2,1)}, f32[16,16,512]{2,1,0:T(8,128)}, f32[64,256]{1,0:T(8,128)}, bf16[592,384]{1,0:T(8,128)(2,1)}, bf16[592,384]{1,...) custom-call(s32[72]{0:T(128)} %refs_0_.1, s32[1,9]{1,0:T(1,128)} %refs_1_.1, ...), custom_call_target="tpu_custom_call" | custom-call | flops 135092560 | bytes 6754628 | tf_op jit(solution)/shard_map/pallas_call | solution.py:920
  8.0 2.4 %collective-permute-start = (bf16[592,384]{1,0:T(8,128)(2,1)}, bf16[592,384]{1,0:T(8,128)(2,1)S(1)}, u32[]{:S(2)}, u32[]{:S(2)}) collective-permute-start(bf16[592,384]{1,0:T(8,128)(2,1)} %get-tuple-element.50), channel_id=1, source_target_pairs={{0,8},{8,16},{16,24},{1,9},{9,17},{17,25},{2,10},{10,18},{18,26},{... | collective-permute-start | bytes 1363976 | tf_op jit(solution)/shard_map/ppermute | solution.py:939
  10.4 1.3 collective-permute-start.1
  12.0 4.4 %collective-permute-done.1.zh.refs_2_.refs_3_.refs_7_ = bf16[592,384]{1,0:T(8,128)(2,1)S(1)} collective-permute-done((bf16[592,384]{1,0:T(8,128)(2,1)}, bf16[592,384]{1,0:T(8,128)(2,1)S(1)}, u32[]{:S(2)}, u32[]{:S(2)}) %collective-permute-start.1) | collective-permute-done | bytes 454688 | tf_op jit(solution)/shard_map/ppermute | solution.py:939
  16.5 0.8 copy-done.1
  17.3 2.7 %shard_map.69 = (f32[24,16,512]{2,1,0:T(8,128)}, bf16[592,384]{1,0:T(8,128)(2,1)}, bf16[592,384]{1,0:T(8,128)(2,1)}) custom-call(bf16[272,384]{1,0:T(8,128)(2,1)} %get-tuple-element.45.own.refs_0_, f32[16,16,512]{2,1,0:T(8,128)} %get-tuple-element.46.r1, f32[64,256]{1,0:T(8,128)} %get-tuple-element.47.r2.refs_2_.refs_5_, ...), custom_call_target="tpu_custom_call" | custom-call | flops 73318400 | bytes 3665920 | tf_op jit(solution)/shard_map/pallas_call | solution.py:920
  20.0 3.4 %collective-permute-start.2 = (bf16[592,384]{1,0:T(8,128)(2,1)}, bf16[592,384]{1,0:T(8,128)(2,1)S(1)}, u32[]{:S(2)}, u32[]{:S(2)}) collective-permute-start(bf16[592,384]{1,0:T(8,128)(2,1)} %get-tuple-element.52), channel_id=1, source_target_pairs={{0,1},{1,2},{2,3},{3,4},{4,5},{5,6},{6,7},{8,9},{9,10},{10,11},{11... | collective-permute-start | bytes 1363976 | tf_op jit(solution)/shard_map/ppermute | solution.py:939
  23.4 1.3 collective-permute-start.3
  24.7 12.2 %shard_map.70 = (f32[32,32,1024]{2,1,0:T(8,128)}, f32[36,32,1024]{2,1,0:T(8,128)}, f32[34,32,1024]{2,1,0:T(8,128)}, f32[32,8,1024]{2,1,0:T(8,128)}) custom-call(bf16[272,384]{1,0:T(8,128)(2,1)} %get-tuple-element.45.own.refs_0_, bf16[592,384]{1,0:T(8,128)(2,1)} %copy-done, bf16[592,384]{1,0:T(8,128)(2,1)} %copy-done.1, f32[32,32,1024]{2,1,0:T(8,128)} %refs_3_.3, ...), custom_call_target="tpu_custom_call" | custom-call | flops 478494720 | bytes 23924736 | tf_op jit(solution)/shard_map/pallas_call | solution.py:920
  37.0 2.6 %collective-permute-done.2.refs_0_.refs_5_ = bf16[592,384]{1,0:T(8,128)(2,1)S(1)} collective-permute-done((bf16[592,384]{1,0:T(8,128)(2,1)}, bf16[592,384]{1,0:T(8,128)(2,1)S(1)}, u32[]{:S(2)}, u32[]{:S(2)}) %collective-permute-start.2) | collective-permute-done | bytes 454688 | tf_op jit(solution)/shard_map/ppermute | solution.py:939
  39.6 0.8 copy-done.4
  40.6 20.9 %shard_map.71 = (f32[20,24,512]{2,1,0:T(8,128)}, bf16[224,512]{1,0:T(8,128)(2,1)}, bf16[224,512]{1,0:T(8,128)(2,1)}, f32[36,40,1024]{2,1,0:T(8,128)}, f32[36,40,1024]{2,1,0:T(8,128)}, /*index=5*/f32[32,32,1024]{2,1,0:T(8,128)}) custom-call(bf16[592,384]{1,0:T(8,128)(2,1)} %copy-done.4, bf16[592,384]{1,0:T(8,128)(2,1)} %copy-done.5, ...), custom_call_target="tpu_custom_call" | custom-call | flops 772997120 | bytes 38649856 | tf_op jit(solution)/shard_map/pallas_call | solution.py:920
  61.4 4.4 %collective-permute-start.4 = (bf16[224,512]{1,0:T(8,128)(2,1)}, bf16[224,512]{1,0:T(8,128)(2,1)S(1)}, u32[]{:S(2)}, u32[]{:S(2)}) collective-permute-start(bf16[224,512]{1,0:T(8,128)(2,1)} %get-tuple-element.68), channel_id=1, source_target_pairs={{0,1},{1,2},{2,3},{3,4},{4,5},{5,6},{6,7},{8,9},{9,10},{10,11},{11... | collective-permute-start | bytes 688136 | tf_op jit(solution)/shard_map/ppermute | solution.py:939
  65.9 1.3 collective-permute-start.5
  67.2 4.8 %shard_map.72 = (bf16[208,1024]{1,0:T(8,128)(2,1)}, bf16[208,1024]{1,0:T(8,128)(2,1)}, bf16[176,1024]{1,0:T(8,128)(2,1)}, bf16[176,1024]{1,0:T(8,128)(2,1)}, bf1...) custom-call(f32[36,40,1024]{2,1,0:T(8,128)} %get-tuple-element.61.v_in.refs_15_, ...), custom_call_target="tpu_custom_call" | custom-call | flops 235929600 | bytes 11796480 | tf_op jit(solution)/shard_map/pallas_call | solution.py:920
  72.1 8.1 %collective-permute-done.5.refs_8_ = bf16[224,512]{1,0:T(8,128)(2,1)S(1)} collective-permute-done((bf16[224,512]{1,0:T(8,128)(2,1)}, bf16[224,512]{1,0:T(8,128)(2,1)S(1)}, u32[]{:S(2)}, u32[]{:S(2)}) %collective-permute-start.5) | collective-permute-done | bytes 229408 | tf_op jit(solution)/shard_map/ppermute | solution.py:939
  80.1 0.7 copy-done.11
  80.8 7.8 %shard_map.73 = (f32[24,24,512]{2,1,0:T(8,128)}, f32[24,24,512]{2,1,0:T(8,128)}, f32[24,24,512]{2,1,0:T(8,128)}, f32[96,256]{1,0:T(8,128)}, bf16[768,512]{1,0:T(...) custom-call(f32[20,24,512]{2,1,0:T(8,128)} %get-tuple-element.60.refs_0_, ...), custom_call_target="tpu_custom_call" | custom-call | flops 171376640 | bytes 8568832 | tf_op jit(solution)/shard_map/pallas_call | solution.py:920
  88.6 1.8 %collective-permute-start.6 = (bf16[768,512]{1,0:T(8,128)(2,1)}, bf16[768,512]{1,0:T(8,128)(2,1)S(1)}, u32[]{:S(2)}, u32[]{:S(2)}) collective-permute-start(bf16[768,512]{1,0:T(8,128)(2,1)} %get-tuple-element.75), channel_id=1, source_target_pairs={{0,8},{8,16},{16,24},{1,9},{9,17},{17,25},{2,10},{10,18},{18,26},{... | collective-permute-start | bytes 2359304 | tf_op jit(solution)/shard_map/ppermute | solution.py:939
  90.4 1.3 collective-permute-start.7
  91.7 4.4 %collective-permute-start.8 = (bf16[176,1024]{1,0:T(8,128)(2,1)}, bf16[176,1024]{1,0:T(8,128)(2,1)S(1)}, u32[]{:S(2)}, u32[]{:S(2)}) collective-permute-start(bf16[176,1024]{1,0:T(8,128)(2,1)} %get-tuple-element.77), channel_id=1, source_target_pairs={{0,1},{1,2},{2,3},{3,4},{4,5},{5,6},{6,7},{8,9},{9,10},{10,11},{11... | collective-permute-start | bytes 1081352 | tf_op jit(solution)/shard_map/ppermute | solution.py:939
  96.1 1.5 collective-permute-start.9
  97.5 2.3 %collective-permute-start.10 = (bf16[80,256]{1,0:T(8,128)(2,1)}, bf16[80,256]{1,0:T(8,128)(2,1)S(1)}, u32[]{:S(2)}, u32[]{:S(2)}) collective-permute-start(bf16[80,256]{1,0:T(8,128)(2,1)} %get-tuple-element.80), channel_id=1, source_target_pairs={{0,16},{8,24},{16,0},{24,8},{1,17},{9,25},{17,1},{25,9},{2,18},{10... | collective-permute-start | bytes 122888 | tf_op jit(solution)/shard_map/ppermute | solution.py:946
  99.8 5.1 %collective-permute-done.10.refs_3_.refs_4_ = bf16[80,256]{1,0:T(8,128)(2,1)S(1)} collective-permute-done((bf16[80,256]{1,0:T(8,128)(2,1)}, bf16[80,256]{1,0:T(8,128)(2,1)S(1)}, u32[]{:S(2)}, u32[]{:S(2)}) %collective-permute-start.10) | collective-permute-done | bytes 40992 | tf_op jit(solution)/shard_map/ppermute | solution.py:946
  106.1 2.7 %shard_map.74 = (f32[32,8,256]{2,1,0:T(8,128)}, f32[32,8,256]{2,1,0:T(8,128)}, bf16[448,256]{1,0:T(8,128)(2,1)}, bf16[448,256]{1,0:T(8,128)(2,1)}, bf16[256,256]{1,0:T(8,128)(2,1)}, /*index=5*/bf16[256,256]{1,0:T(8,128)(2,1)}) custom-call(f32[96,256]{1,0:T(8,128)} %get-tuple-element.79.refs_0_, bf16[768,512]{1,0:T(8,128)(2,1)} %copy-done.2, ...), custom_call_target="tpu_custom_call" | custom-call | flops 79462400 | bytes 3973120 | tf_op jit(solution)/shard_map/pallas_call | solution.py:920
  108.8 4.3 %collective-permute-start.11 = (bf16[448,256]{1,0:T(8,128)(2,1)}, bf16[448,256]{1,0:T(8,128)(2,1)S(1)}, u32[]{:S(2)}, u32[]{:S(2)}) collective-permute-start(bf16[448,256]{1,0:T(8,128)(2,1)} %get-tuple-element.82), channel_id=1, source_target_pairs={{0,1},{1,2},{2,3},{3,4},{4,5},{5,6},{6,7},{8,9},{9,10},{10,11},{11... | collective-permute-start | bytes 688136 | tf_op jit(solution)/shard_map/ppermute | solution.py:939
  113.2 1.3 collective-permute-start.12
  114.5 7.7 %collective-permute-start.13 = (bf16[256,256]{1,0:T(8,128)(2,1)}, bf16[256,256]{1,0:T(8,128)(2,1)S(1)}, u32[]{:S(2)}, u32[]{:S(2)}) collective-permute-start(bf16[256,256]{1,0:T(8,128)(2,1)} %get-tuple-element.84), channel_id=1, source_target_pairs={{0,2},{1,3},{2,4},{3,5},{4,6},{5,7},{8,10},{9,11},{10,12},{11,13},... | collective-permute-start | bytes 393224 | tf_op jit(solution)/shard_map/ppermute | solution.py:939
  122.2 1.3 collective-permute-start.14
  123.5 1.5 collective-permute-done.13.refs_12_
  125.0 4.3 %collective-permute-done.14.refs_13_ = bf16[256,256]{1,0:T(8,128)(2,1)S(1)} collective-permute-done((bf16[256,256]{1,0:T(8,128)(2,1)}, bf16[256,256]{1,0:T(8,128)(2,1)S(1)}, u32[]{:S(2)}, u32[]{:S(2)}) %collective-permute-start.14) | collective-permute-done | bytes 131104 | tf_op jit(solution)/shard_map/ppermute | solution.py:939
  130.1 22.9 %shard_map.75 = f32[32,32,1024]{2,1,0:T(8,128)} custom-call(f32[24,24,512]{2,1,0:T(8,128)} %get-tuple-element.72.refs_0_, f32[24,24,512]{2,1,0:T(8,128)} %get-tuple-element.73.refs_1_, f32[24,24,512]{2,1,0:T(8,128)} %get-tuple-element.74.refs_2_, bf16[768,512]{1,0:T(8,128)(2,1)} %copy-done.2, bf16[768,512]{1,0:T(8,128)(2,1)} %copy-done.3, ...), custom_call_target="tpu_custom_call" | custom-call | flops 563445760 | bytes 28172288 | tf_op jit(solution)/shard_map/pallas_call | solution.py:920
  (36 shorter events, 2.5 us)
Async XLA Ops:
  8.0 4.0 %collective-permute-start = (bf16[592,384]{1,0:T(8,128)(2,1)}, bf16[592,384]{1,0:T(8,128)(2,1)S(1)}, u32[]{:S(2)}, u32[]{:S(2)}) collective-permute-start(bf16[592,384]{1,0:T(8,128)(2,1)} %get-tuple-element.50), channel_id=1, source_target_pairs={{0,8},{8,16},{16,24},{1,9},{9,17},{17,25},{2,10},{10,18},{18,26},{... | collective-permute-start | bytes 1363976 | tf_op jit(solution)/shard_map/ppermute | solution.py:939
  10.4 6.0 %collective-permute-start.1 = (bf16[592,384]{1,0:T(8,128)(2,1)}, bf16[592,384]{1,0:T(8,128)(2,1)S(1)}, u32[]{:S(2)}, u32[]{:S(2)}) collective-permute-start(bf16[592,384]{1,0:T(8,128)(2,1)} %get-tuple-element.51), channel_id=1, source_target_pairs={{8,0},{16,8},{24,16},{9,1},{17,9},{25,17},{10,2},{18,10},{26,18},{... | collective-permute-start | bytes 1363976 | tf_op jit(solution)/shard_map/ppermute | solution.py:939
  12.0 4.4 %copy-start = (bf16[592,384]{1,0:T(8,128)(2,1)}, bf16[592,384]{1,0:T(8,128)(2,1)S(1)}, u32[]{:S(2)}) copy-start(bf16[592,384]{1,0:T(8,128)(2,1)S(1)} %collective-permute-done.zl.refs_1_.refs_2_.refs_6_) | copy-start | bytes 1363972
  16.5 0.8 copy-start.1
  20.0 19.6 %collective-permute-start.2 = (bf16[592,384]{1,0:T(8,128)(2,1)}, bf16[592,384]{1,0:T(8,128)(2,1)S(1)}, u32[]{:S(2)}, u32[]{:S(2)}) collective-permute-start(bf16[592,384]{1,0:T(8,128)(2,1)} %get-tuple-element.52), channel_id=1, source_target_pairs={{0,1},{1,2},{2,3},{3,4},{4,5},{5,6},{6,7},{8,9},{9,10},{10,11},{11... | collective-permute-start | bytes 1363976 | tf_op jit(solution)/shard_map/ppermute | solution.py:939
  23.4 16.2 %collective-permute-start.3 = (bf16[592,384]{1,0:T(8,128)(2,1)}, bf16[592,384]{1,0:T(8,128)(2,1)S(1)}, u32[]{:S(2)}, u32[]{:S(2)}) collective-permute-start(bf16[592,384]{1,0:T(8,128)(2,1)} %get-tuple-element.53), channel_id=1, source_target_pairs={{1,0},{2,1},{3,2},{4,3},{5,4},{6,5},{7,6},{9,8},{10,9},{11,10},{12... | collective-permute-start | bytes 1363976 | tf_op jit(solution)/shard_map/ppermute | solution.py:939
  39.6 0.8 copy-start.4
  39.6 1.0 copy-start.5
  61.4 10.6 %collective-permute-start.4 = (bf16[224,512]{1,0:T(8,128)(2,1)}, bf16[224,512]{1,0:T(8,128)(2,1)S(1)}, u32[]{:S(2)}, u32[]{:S(2)}) collective-permute-start(bf16[224,512]{1,0:T(8,128)(2,1)} %get-tuple-element.68), channel_id=1, source_target_pairs={{0,1},{1,2},{2,3},{3,4},{4,5},{5,6},{6,7},{8,9},{9,10},{10,11},{11... | collective-permute-start | bytes 688136 | tf_op jit(solution)/shard_map/ppermute | solution.py:939
  65.9 14.2 %collective-permute-start.5 = (bf16[224,512]{1,0:T(8,128)(2,1)}, bf16[224,512]{1,0:T(8,128)(2,1)S(1)}, u32[]{:S(2)}, u32[]{:S(2)}) collective-permute-start(bf16[224,512]{1,0:T(8,128)(2,1)} %get-tuple-element.69), channel_id=1, source_target_pairs={{1,0},{2,1},{3,2},{4,3},{5,4},{6,5},{7,6},{9,8},{10,9},{11,10},{12... | collective-permute-start | bytes 688136 | tf_op jit(solution)/shard_map/ppermute | solution.py:939
  72.0 8.1 %copy-start.10 = (bf16[224,512]{1,0:T(8,128)(2,1)}, bf16[224,512]{1,0:T(8,128)(2,1)S(1)}, u32[]{:S(2)}) copy-start(bf16[224,512]{1,0:T(8,128)(2,1)S(1)} %collective-permute-done.4.refs_7_) | copy-start | bytes 688132
  80.1 0.7 copy-start.11
  88.6 16.3 %collective-permute-start.6 = (bf16[768,512]{1,0:T(8,128)(2,1)}, bf16[768,512]{1,0:T(8,128)(2,1)S(1)}, u32[]{:S(2)}, u32[]{:S(2)}) collective-permute-start(bf16[768,512]{1,0:T(8,128)(2,1)} %get-tuple-element.75), channel_id=1, source_target_pairs={{0,8},{8,16},{16,24},{1,9},{9,17},{17,25},{2,10},{10,18},{18,26},{... | collective-permute-start | bytes 2359304 | tf_op jit(solution)/shard_map/ppermute | solution.py:939
  90.4 14.6 %collective-permute-start.7 = (bf16[768,512]{1,0:T(8,128)(2,1)}, bf16[768,512]{1,0:T(8,128)(2,1)S(1)}, u32[]{:S(2)}, u32[]{:S(2)}) collective-permute-start(bf16[768,512]{1,0:T(8,128)(2,1)} %get-tuple-element.76), channel_id=1, source_target_pairs={{8,0},{16,8},{24,16},{9,1},{17,9},{25,17},{10,2},{18,10},{26,18},{... | collective-permute-start | bytes 2359304 | tf_op jit(solution)/shard_map/ppermute | solution.py:939
  91.7 30.5 %collective-permute-start.8 = (bf16[176,1024]{1,0:T(8,128)(2,1)}, bf16[176,1024]{1,0:T(8,128)(2,1)S(1)}, u32[]{:S(2)}, u32[]{:S(2)}) collective-permute-start(bf16[176,1024]{1,0:T(8,128)(2,1)} %get-tuple-element.77), channel_id=1, source_target_pairs={{0,1},{1,2},{2,3},{3,4},{4,5},{5,6},{6,7},{8,9},{9,10},{10,11},{11... | collective-permute-start | bytes 1081352 | tf_op jit(solution)/shard_map/ppermute | solution.py:939
  96.1 27.5 %collective-permute-start.9 = (bf16[176,1024]{1,0:T(8,128)(2,1)}, bf16[176,1024]{1,0:T(8,128)(2,1)S(1)}, u32[]{:S(2)}, u32[]{:S(2)}) collective-permute-start(bf16[176,1024]{1,0:T(8,128)(2,1)} %get-tuple-element.78), channel_id=1, source_target_pairs={{1,0},{2,1},{3,2},{4,3},{5,4},{6,5},{7,6},{9,8},{10,9},{11,10},{12... | collective-permute-start | bytes 1081352 | tf_op jit(solution)/shard_map/ppermute | solution.py:939
  97.5 7.4 %collective-permute-start.10 = (bf16[80,256]{1,0:T(8,128)(2,1)}, bf16[80,256]{1,0:T(8,128)(2,1)S(1)}, u32[]{:S(2)}, u32[]{:S(2)}) collective-permute-start(bf16[80,256]{1,0:T(8,128)(2,1)} %get-tuple-element.80), channel_id=1, source_target_pairs={{0,16},{8,24},{16,0},{24,8},{1,17},{9,25},{17,1},{25,9},{2,18},{10... | collective-permute-start | bytes 122888 | tf_op jit(solution)/shard_map/ppermute | solution.py:946
  104.9 0.6 copy-start.12
  104.9 0.9 copy-start.2
  104.9 1.1 copy-start.3
  108.8 20.5 %collective-permute-start.11 = (bf16[448,256]{1,0:T(8,128)(2,1)}, bf16[448,256]{1,0:T(8,128)(2,1)S(1)}, u32[]{:S(2)}, u32[]{:S(2)}) collective-permute-start(bf16[448,256]{1,0:T(8,128)(2,1)} %get-tuple-element.82), channel_id=1, source_target_pairs={{0,1},{1,2},{2,3},{3,4},{4,5},{5,6},{6,7},{8,9},{9,10},{10,11},{11... | collective-permute-start | bytes 688136 | tf_op jit(solution)/shard_map/ppermute | solution.py:939
  113.2 16.1 %collective-permute-start.12 = (bf16[448,256]{1,0:T(8,128)(2,1)}, bf16[448,256]{1,0:T(8,128)(2,1)S(1)}, u32[]{:S(2)}, u32[]{:S(2)}) collective-permute-start(bf16[448,256]{1,0:T(8,128)(2,1)} %get-tuple-element.83), channel_id=1, source_target_pairs={{1,0},{2,1},{3,2},{4,3},{5,4},{6,5},{7,6},{9,8},{10,9},{11,10},{12... | collective-permute-start | bytes 688136 | tf_op jit(solution)/shard_map/ppermute | solution.py:939
  114.5 10.5 %collective-permute-start.13 = (bf16[256,256]{1,0:T(8,128)(2,1)}, bf16[256,256]{1,0:T(8,128)(2,1)S(1)}, u32[]{:S(2)}, u32[]{:S(2)}) collective-permute-start(bf16[256,256]{1,0:T(8,128)(2,1)} %get-tuple-element.84), channel_id=1, source_target_pairs={{0,2},{1,3},{2,4},{3,5},{4,6},{5,7},{8,10},{9,11},{10,12},{11,13},... | collective-permute-start | bytes 393224 | tf_op jit(solution)/shard_map/ppermute | solution.py:939
  122.2 7.1 %copy-start.6 = (bf16[176,1024]{1,0:T(8,128)(2,1)}, bf16[176,1024]{1,0:T(8,128)(2,1)S(1)}, u32[]{:S(2)}) copy-start(bf16[176,1024]{1,0:T(8,128)(2,1)S(1)} %collective-permute-done.8.refs_7_) | copy-start | bytes 1081348
  122.2 7.1 %collective-permute-start.14 = (bf16[256,256]{1,0:T(8,128)(2,1)}, bf16[256,256]{1,0:T(8,128)(2,1)S(1)}, u32[]{:S(2)}, u32[]{:S(2)}) collective-permute-start(bf16[256,256]{1,0:T(8,128)(2,1)} %get-tuple-element.85), channel_id=1, source_target_pairs={{2,0},{3,1},{4,2},{5,3},{6,4},{7,5},{10,8},{11,9},{12,10},{13,11},... | collective-permute-start | bytes 393224 | tf_op jit(solution)/shard_map/ppermute | solution.py:939
  123.5 5.8 %copy-start.7 = (bf16[176,1024]{1,0:T(8,128)(2,1)}, bf16[176,1024]{1,0:T(8,128)(2,1)S(1)}, u32[]{:S(2)}) copy-start(bf16[176,1024]{1,0:T(8,128)(2,1)S(1)} %collective-permute-done.9.refs_8_) | copy-start | bytes 1081348
  125.0 4.3 %copy-start.13 = (bf16[256,256]{1,0:T(8,128)(2,1)}, bf16[256,256]{1,0:T(8,128)(2,1)S(1)}, u32[]{:S(2)}) copy-start(bf16[256,256]{1,0:T(8,128)(2,1)S(1)} %collective-permute-done.13.refs_12_) | copy-start | bytes 393220
  129.3 0.7 copy-start.14
  129.3 0.8 copy-start.8
  129.3 0.8 copy-start.9

commit v3 on v2

--- a/solution.py
+++ b/solution.py
@@ -376,7 +376,7 @@
             v1[z + 1, :, lanes(t)] = KEEP * here[0:32] + g0[z + Q, :, lanes(t)] * body
             edge[z, :, lanes(t)] = inner[32:40]
 
-    loop(0, C, first, 2)
+    loop(0, C, first, 4)
     for z in (-1, C):
         for t in range(NT):
             near = va[z + O + (1 if z < 0 else -1), 0:32, lanes(t)]
@@ -460,7 +460,7 @@
 
     loop(0, C, edges)
 
-    loop(0, C, lambda z: sweep(vb, va, supply, gg, z, True), 2)
+    loop(0, C, lambda z: sweep(vb, va, supply, gg, z, True), 4)
     loop(0, 4, lambda i: sweep(vb, va, supply, gg, jnp.where(i < 2, i - 2, i + C - 2), False))
     loads[4].wait()
     v_copy = pltpu.make_async_copy(va.at[3:39], v_out, sems.at[5])
@@ -490,7 +490,7 @@
         zs = (2 * m - 4, 2 * m - 3)
         coarse(m, zs, [lambda t, z=z: upt[z, :, lanes(t)] for z in zs], True)
 
-    loop(2, 18, inner)
+    loop(2, 18, inner, 2)
     for m, ref, z in ((1, zl, -2), (18, zh, C)):
         coarse(m, (z, z + 1), [from_message(ref, 0), from_message(ref, 1)], False)
 
@@ -887,7 +887,7 @@
                 vb[z + 1, 0:32, lanes(t)] = KEEP * here[0:32] + g[0:32] * (supply[z, :, lanes(t)] + inner[0:32])
                 vb[z + 1, 32:40, lanes(t)] = KEEP * here[32:40] + g[32:40] * (f + inner[32:40])
 
-        loop(0, 16, step, 2)
+        loop(0, 16, step, 4)
 
     loop(0, 2, first)
     for p, ref in ((1, zsl), (34, zsh)):
@@ -903,7 +903,7 @@
     stores = []
     for i in range(4):
         part = pl.ds(8 * i, 8)
-        loop(8 * i, 8 * i + 8, second, 2)
+        loop(8 * i, 8 * i + 8, second, 4)
         stores.append(pltpu.make_async_copy(out.at[part], out_hbm.at[part], sems.at[3 + i]))
         stores[i].start()
     for copy in stores:

time: 154 us -> 152 us (0.987)
  Pallas kernels: 81.5 us -> 78.9 us
    pallas_call x8, Pallas kernels: 81.5 us -> 78.9 us  [call(): pl.pallas_call(kernel, out_shape=tuple(outs), in_specs=[SMEM] * smem + [V...]
where the time goes in v3:
time: 152 us; the launch traced here: 151 us
  Pallas kernels  78.9 us (52%)
  starting transfers between devices  39.9 us (26%)
  waiting for transfers between devices  26.9 us (18%)
  local copies, waits for them, and re-layouts  4.39 us (3%)
    pallas_call x8, Pallas kernels, call(): pl.pallas_call(kernel, out_shape=tuple(outs), in_specs=[SMEM] * smem + [V...  78.9 us
    ppermute x14, starting transfers between devices, both_ways(): return (lax.ppermute(to_high, axis, up), lax.ppermute(to_low, axis, down))  37.7 us
    ppermute x14, waiting for transfers between devices, both_ways(): return (lax.ppermute(to_high, axis, up), lax.ppermute(to_low, axis, down))  21.6 us
    ppermute x1, waiting for transfers between devices, two_away(): came = lax.ppermute(to_low, 'gz', [(i, (i + 2) % 4) for i in range(4)])  5.29 us
    unnamed x30, local copies, waits for them, and re-layouts  4.39 us
  transfers between devices with their start and end apart: 15, of which 7 were waited for; matrix products, arithmetic and copies ran while one was open for 0% of the time, Pallas kernels for 13%

profile of v3, /device:TPU:0, one launch (start us, length us, event | category | flops | bytes accessed | tf_op | source)
XLA Modules:
  0.0 151.2 jit_solution(10402727763720012259)
XLA Ops:
  0.6 7.4 %shard_map.68 = (bf16[272,384]{1,0:T(8,128)(2,1)}, f32[16,16,512]{2,1,0:T(8,128)}, f32[64,256]{1,0:T(8,128)}, bf16[592,384]{1,0:T(8,128)(2,1)}, bf16[592,384]{1,...) custom-call(s32[72]{0:T(128)} %refs_0_.1, s32[1,9]{1,0:T(1,128)} %refs_1_.1, ...), custom_call_target="tpu_custom_call" | custom-call | flops 135092560 | bytes 6754628 | tf_op jit(solution)/shard_map/pallas_call | solution.py:920
  8.0 2.4 %collective-permute-start = (bf16[592,384]{1,0:T(8,128)(2,1)}, bf16[592,384]{1,0:T(8,128)(2,1)S(1)}, u32[]{:S(2)}, u32[]{:S(2)}) collective-permute-start(bf16[592,384]{1,0:T(8,128)(2,1)} %get-tuple-element.50), channel_id=1, source_target_pairs={{0,8},{8,16},{16,24},{1,9},{9,17},{17,25},{2,10},{10,18},{18,26},{... | collective-permute-start | bytes 1363976 | tf_op jit(solution)/shard_map/ppermute | solution.py:939
  10.4 1.3 collective-permute-start.1
  12.0 4.4 %collective-permute-done.1.zh.refs_2_.refs_3_.refs_7_ = bf16[592,384]{1,0:T(8,128)(2,1)S(1)} collective-permute-done((bf16[592,384]{1,0:T(8,128)(2,1)}, bf16[592,384]{1,0:T(8,128)(2,1)S(1)}, u32[]{:S(2)}, u32[]{:S(2)}) %collective-permute-start.1) | collective-permute-done | bytes 454688 | tf_op jit(solution)/shard_map/ppermute | solution.py:939
  16.5 0.8 copy-done.1
  17.3 2.7 %shard_map.69 = (f32[24,16,512]{2,1,0:T(8,128)}, bf16[592,384]{1,0:T(8,128)(2,1)}, bf16[592,384]{1,0:T(8,128)(2,1)}) custom-call(bf16[272,384]{1,0:T(8,128)(2,1)} %get-tuple-element.45.own.refs_0_, f32[16,16,512]{2,1,0:T(8,128)} %get-tuple-element.46.r1, f32[64,256]{1,0:T(8,128)} %get-tuple-element.47.r2.refs_2_.refs_5_, ...), custom_call_target="tpu_custom_call" | custom-call | flops 73318400 | bytes 3665920 | tf_op jit(solution)/shard_map/pallas_call | solution.py:920
  20.0 3.4 %collective-permute-start.2 = (bf16[592,384]{1,0:T(8,128)(2,1)}, bf16[592,384]{1,0:T(8,128)(2,1)S(1)}, u32[]{:S(2)}, u32[]{:S(2)}) collective-permute-start(bf16[592,384]{1,0:T(8,128)(2,1)} %get-tuple-element.52), channel_id=1, source_target_pairs={{0,1},{1,2},{2,3},{3,4},{4,5},{5,6},{6,7},{8,9},{9,10},{10,11},{11... | collective-permute-start | bytes 1363976 | tf_op jit(solution)/shard_map/ppermute | solution.py:939
  23.4 1.3 collective-permute-start.3
  24.7 11.6 %shard_map.70 = (f32[32,32,1024]{2,1,0:T(8,128)}, f32[36,32,1024]{2,1,0:T(8,128)}, f32[34,32,1024]{2,1,0:T(8,128)}, f32[32,8,1024]{2,1,0:T(8,128)}) custom-call(bf16[272,384]{1,0:T(8,128)(2,1)} %get-tuple-element.45.own.refs_0_, bf16[592,384]{1,0:T(8,128)(2,1)} %copy-done, bf16[592,384]{1,0:T(8,128)(2,1)} %copy-done.1, f32[32,32,1024]{2,1,0:T(8,128)} %refs_3_.3, ...), custom_call_target="tpu_custom_call" | custom-call | flops 478494720 | bytes 23924736 | tf_op jit(solution)/shard_map/pallas_call | solution.py:920
  36.4 3.2 %collective-permute-done.2.refs_0_.refs_5_ = bf16[592,384]{1,0:T(8,128)(2,1)S(1)} collective-permute-done((bf16[592,384]{1,0:T(8,128)(2,1)}, bf16[592,384]{1,0:T(8,128)(2,1)S(1)}, u32[]{:S(2)}, u32[]{:S(2)}) %collective-permute-start.2) | collective-permute-done | bytes 454688 | tf_op jit(solution)/shard_map/ppermute | solution.py:939
  39.6 0.8 copy-done.4
  40.6 19.9 %shard_map.71 = (f32[20,24,512]{2,1,0:T(8,128)}, bf16[224,512]{1,0:T(8,128)(2,1)}, bf16[224,512]{1,0:T(8,128)(2,1)}, f32[36,40,1024]{2,1,0:T(8,128)}, f32[36,40,1024]{2,1,0:T(8,128)}, /*index=5*/f32[32,32,1024]{2,1,0:T(8,128)}) custom-call(bf16[592,384]{1,0:T(8,128)(2,1)} %copy-done.4, bf16[592,384]{1,0:T(8,128)(2,1)} %copy-done.5, ...), custom_call_target="tpu_custom_call" | custom-call | flops 772997120 | bytes 38649856 | tf_op jit(solution)/shard_map/pallas_call | solution.py:920
  60.4 4.4 %collective-permute-start.4 = (bf16[224,512]{1,0:T(8,128)(2,1)}, bf16[224,512]{1,0:T(8,128)(2,1)S(1)}, u32[]{:S(2)}, u32[]{:S(2)}) collective-permute-start(bf16[224,512]{1,0:T(8,128)(2,1)} %get-tuple-element.68), channel_id=1, source_target_pairs={{0,1},{1,2},{2,3},{3,4},{4,5},{5,6},{6,7},{8,9},{9,10},{10,11},{11... | collective-permute-start | bytes 688136 | tf_op jit(solution)/shard_map/ppermute | solution.py:939
  64.9 1.5 collective-permute-start.5
  66.3 4.8 %shard_map.72 = (bf16[208,1024]{1,0:T(8,128)(2,1)}, bf16[208,1024]{1,0:T(8,128)(2,1)}, bf16[176,1024]{1,0:T(8,128)(2,1)}, bf16[176,1024]{1,0:T(8,128)(2,1)}, bf1...) custom-call(f32[36,40,1024]{2,1,0:T(8,128)} %get-tuple-element.61.v_in.refs_15_, ...), custom_call_target="tpu_custom_call" | custom-call | flops 235929600 | bytes 11796480 | tf_op jit(solution)/shard_map/pallas_call | solution.py:920
  71.2 7.9 %collective-permute-done.5.refs_8_ = bf16[224,512]{1,0:T(8,128)(2,1)S(1)} collective-permute-done((bf16[224,512]{1,0:T(8,128)(2,1)}, bf16[224,512]{1,0:T(8,128)(2,1)S(1)}, u32[]{:S(2)}, u32[]{:S(2)}) %collective-permute-start.5) | collective-permute-done | bytes 229408 | tf_op jit(solution)/shard_map/ppermute | solution.py:939
  79.1 0.7 copy-done.11
  79.8 7.8 %shard_map.73 = (f32[24,24,512]{2,1,0:T(8,128)}, f32[24,24,512]{2,1,0:T(8,128)}, f32[24,24,512]{2,1,0:T(8,128)}, f32[96,256]{1,0:T(8,128)}, bf16[768,512]{1,0:T(...) custom-call(f32[20,24,512]{2,1,0:T(8,128)} %get-tuple-element.60.refs_0_, ...), custom_call_target="tpu_custom_call" | custom-call | flops 171376640 | bytes 8568832 | tf_op jit(solution)/shard_map/pallas_call | solution.py:920
  87.6 1.8 %collective-permute-start.6 = (bf16[768,512]{1,0:T(8,128)(2,1)}, bf16[768,512]{1,0:T(8,128)(2,1)S(1)}, u32[]{:S(2)}, u32[]{:S(2)}) collective-permute-start(bf16[768,512]{1,0:T(8,128)(2,1)} %get-tuple-element.75), channel_id=1, source_target_pairs={{0,8},{8,16},{16,24},{1,9},{9,17},{17,25},{2,10},{10,18},{18,26},{... | collective-permute-start | bytes 2359304 | tf_op jit(solution)/shard_map/ppermute | solution.py:939
  89.4 1.3 collective-permute-start.7
  90.7 4.4 %collective-permute-start.8 = (bf16[176,1024]{1,0:T(8,128)(2,1)}, bf16[176,1024]{1,0:T(8,128)(2,1)S(1)}, u32[]{:S(2)}, u32[]{:S(2)}) collective-permute-start(bf16[176,1024]{1,0:T(8,128)(2,1)} %get-tuple-element.77), channel_id=1, source_target_pairs={{0,1},{1,2},{2,3},{3,4},{4,5},{5,6},{6,7},{8,9},{9,10},{10,11},{11... | collective-permute-start | bytes 1081352 | tf_op jit(solution)/shard_map/ppermute | solution.py:939
  95.1 1.3 collective-permute-start.9
  96.4 2.3 %collective-permute-start.10 = (bf16[80,256]{1,0:T(8,128)(2,1)}, bf16[80,256]{1,0:T(8,128)(2,1)S(1)}, u32[]{:S(2)}, u32[]{:S(2)}) collective-permute-start(bf16[80,256]{1,0:T(8,128)(2,1)} %get-tuple-element.80), channel_id=1, source_target_pairs={{0,16},{8,24},{16,0},{24,8},{1,17},{9,25},{17,1},{25,9},{2,18},{10... | collective-permute-start | bytes 122888 | tf_op jit(solution)/shard_map/ppermute | solution.py:946
  98.6 5.3 %collective-permute-done.10.refs_3_.refs_4_ = bf16[80,256]{1,0:T(8,128)(2,1)S(1)} collective-permute-done((bf16[80,256]{1,0:T(8,128)(2,1)}, bf16[80,256]{1,0:T(8,128)(2,1)S(1)}, u32[]{:S(2)}, u32[]{:S(2)}) %collective-permute-start.10) | collective-permute-done | bytes 40992 | tf_op jit(solution)/shard_map/ppermute | solution.py:946
  105.1 2.7 %shard_map.74 = (f32[32,8,256]{2,1,0:T(8,128)}, f32[32,8,256]{2,1,0:T(8,128)}, bf16[448,256]{1,0:T(8,128)(2,1)}, bf16[448,256]{1,0:T(8,128)(2,1)}, bf16[256,256]{1,0:T(8,128)(2,1)}, /*index=5*/bf16[256,256]{1,0:T(8,128)(2,1)}) custom-call(f32[96,256]{1,0:T(8,128)} %get-tuple-element.79.refs_0_, bf16[768,512]{1,0:T(8,128)(2,1)} %copy-done.2, ...), custom_call_target="tpu_custom_call" | custom-call | flops 79462400 | bytes 3973120 | tf_op jit(solution)/shard_map/pallas_call | solution.py:920
  107.8 4.3 %collective-permute-start.11 = (bf16[448,256]{1,0:T(8,128)(2,1)}, bf16[448,256]{1,0:T(8,128)(2,1)S(1)}, u32[]{:S(2)}, u32[]{:S(2)}) collective-permute-start(bf16[448,256]{1,0:T(8,128)(2,1)} %get-tuple-element.82), channel_id=1, source_target_pairs={{0,1},{1,2},{2,3},{3,4},{4,5},{5,6},{6,7},{8,9},{9,10},{10,11},{11... | collective-permute-start | bytes 688136 | tf_op jit(solution)/shard_map/ppermute | solution.py:939
  112.2 1.3 collective-permute-start.12
  113.5 7.7 %collective-permute-start.13 = (bf16[256,256]{1,0:T(8,128)(2,1)}, bf16[256,256]{1,0:T(8,128)(2,1)S(1)}, u32[]{:S(2)}, u32[]{:S(2)}) collective-permute-start(bf16[256,256]{1,0:T(8,128)(2,1)} %get-tuple-element.84), channel_id=1, source_target_pairs={{0,2},{1,3},{2,4},{3,5},{4,6},{5,7},{8,10},{9,11},{10,12},{11,13},... | collective-permute-start | bytes 393224 | tf_op jit(solution)/shard_map/ppermute | solution.py:939
  121.2 1.3 collective-permute-start.14
  122.5 1.5 collective-permute-done.13.refs_12_
  124.0 4.3 %collective-permute-done.14.refs_13_ = bf16[256,256]{1,0:T(8,128)(2,1)S(1)} collective-permute-done((bf16[256,256]{1,0:T(8,128)(2,1)}, bf16[256,256]{1,0:T(8,128)(2,1)S(1)}, u32[]{:S(2)}, u32[]{:S(2)}) %collective-permute-start.14) | collective-permute-done | bytes 131104 | tf_op jit(solution)/shard_map/ppermute | solution.py:939
  129.1 21.9 %shard_map.75 = f32[32,32,1024]{2,1,0:T(8,128)} custom-call(f32[24,24,512]{2,1,0:T(8,128)} %get-tuple-element.72.refs_0_, f32[24,24,512]{2,1,0:T(8,128)} %get-tuple-element.73.refs_1_, f32[24,24,512]{2,1,0:T(8,128)} %get-tuple-element.74.refs_2_, bf16[768,512]{1,0:T(8,128)(2,1)} %copy-done.2, bf16[768,512]{1,0:T(8,128)(2,1)} %copy-done.3, ...), custom_call_target="tpu_custom_call" | custom-call | flops 563445760 | bytes 28172288 | tf_op jit(solution)/shard_map/pallas_call | solution.py:920
  (36 shorter events, 2.5 us)
Async XLA Ops:
  8.0 4.0 %collective-permute-start = (bf16[592,384]{1,0:T(8,128)(2,1)}, bf16[592,384]{1,0:T(8,128)(2,1)S(1)}, u32[]{:S(2)}, u32[]{:S(2)}) collective-permute-start(bf16[592,384]{1,0:T(8,128)(2,1)} %get-tuple-element.50), channel_id=1, source_target_pairs={{0,8},{8,16},{16,24},{1,9},{9,17},{17,25},{2,10},{10,18},{18,26},{... | collective-permute-start | bytes 1363976 | tf_op jit(solution)/shard_map/ppermute | solution.py:939
  10.4 6.0 %collective-permute-start.1 = (bf16[592,384]{1,0:T(8,128)(2,1)}, bf16[592,384]{1,0:T(8,128)(2,1)S(1)}, u32[]{:S(2)}, u32[]{:S(2)}) collective-permute-start(bf16[592,384]{1,0:T(8,128)(2,1)} %get-tuple-element.51), channel_id=1, source_target_pairs={{8,0},{16,8},{24,16},{9,1},{17,9},{25,17},{10,2},{18,10},{26,18},{... | collective-permute-start | bytes 1363976 | tf_op jit(solution)/shard_map/ppermute | solution.py:939
  12.0 4.4 %copy-start = (bf16[592,384]{1,0:T(8,128)(2,1)}, bf16[592,384]{1,0:T(8,128)(2,1)S(1)}, u32[]{:S(2)}) copy-start(bf16[592,384]{1,0:T(8,128)(2,1)S(1)} %collective-permute-done.zl.refs_1_.refs_2_.refs_6_) | copy-start | bytes 1363972
  16.5 0.8 copy-start.1
  20.0 19.6 %collective-permute-start.2 = (bf16[592,384]{1,0:T(8,128)(2,1)}, bf16[592,384]{1,0:T(8,128)(2,1)S(1)}, u32[]{:S(2)}, u32[]{:S(2)}) collective-permute-start(bf16[592,384]{1,0:T(8,128)(2,1)} %get-tuple-element.52), channel_id=1, source_target_pairs={{0,1},{1,2},{2,3},{3,4},{4,5},{5,6},{6,7},{8,9},{9,10},{10,11},{11... | collective-permute-start | bytes 1363976 | tf_op jit(solution)/shard_map/ppermute | solution.py:939
  23.4 16.2 %collective-permute-start.3 = (bf16[592,384]{1,0:T(8,128)(2,1)}, bf16[592,384]{1,0:T(8,128)(2,1)S(1)}, u32[]{:S(2)}, u32[]{:S(2)}) collective-permute-start(bf16[592,384]{1,0:T(8,128)(2,1)} %get-tuple-element.53), channel_id=1, source_target_pairs={{1,0},{2,1},{3,2},{4,3},{5,4},{6,5},{7,6},{9,8},{10,9},{11,10},{12... | collective-permute-start | bytes 1363976 | tf_op jit(solution)/shard_map/ppermute | solution.py:939
  39.6 0.8 copy-start.4
  39.6 1.0 copy-start.5
  60.4 10.8 %collective-permute-start.4 = (bf16[224,512]{1,0:T(8,128)(2,1)}, bf16[224,512]{1,0:T(8,128)(2,1)S(1)}, u32[]{:S(2)}, u32[]{:S(2)}) collective-permute-start(bf16[224,512]{1,0:T(8,128)(2,1)} %get-tuple-element.68), channel_id=1, source_target_pairs={{0,1},{1,2},{2,3},{3,4},{4,5},{5,6},{6,7},{8,9},{9,10},{10,11},{11... | collective-permute-start | bytes 688136 | tf_op jit(solution)/shard_map/ppermute | solution.py:939
  64.9 14.2 %collective-permute-start.5 = (bf16[224,512]{1,0:T(8,128)(2,1)}, bf16[224,512]{1,0:T(8,128)(2,1)S(1)}, u32[]{:S(2)}, u32[]{:S(2)}) collective-permute-start(bf16[224,512]{1,0:T(8,128)(2,1)} %get-tuple-element.69), channel_id=1, source_target_pairs={{1,0},{2,1},{3,2},{4,3},{5,4},{6,5},{7,6},{9,8},{10,9},{11,10},{12... | collective-permute-start | bytes 688136 | tf_op jit(solution)/shard_map/ppermute | solution.py:939
  71.2 7.9 %copy-start.10 = (bf16[224,512]{1,0:T(8,128)(2,1)}, bf16[224,512]{1,0:T(8,128)(2,1)S(1)}, u32[]{:S(2)}) copy-start(bf16[224,512]{1,0:T(8,128)(2,1)S(1)} %collective-permute-done.4.refs_7_) | copy-start | bytes 688132
  79.1 0.7 copy-start.11
  87.6 16.3 %collective-permute-start.6 = (bf16[768,512]{1,0:T(8,128)(2,1)}, bf16[768,512]{1,0:T(8,128)(2,1)S(1)}, u32[]{:S(2)}, u32[]{:S(2)}) collective-permute-start(bf16[768,512]{1,0:T(8,128)(2,1)} %get-tuple-element.75), channel_id=1, source_target_pairs={{0,8},{8,16},{16,24},{1,9},{9,17},{17,25},{2,10},{10,18},{18,26},{... | collective-permute-start | bytes 2359304 | tf_op jit(solution)/shard_map/ppermute | solution.py:939
  89.4 14.6 %collective-permute-start.7 = (bf16[768,512]{1,0:T(8,128)(2,1)}, bf16[768,512]{1,0:T(8,128)(2,1)S(1)}, u32[]{:S(2)}, u32[]{:S(2)}) collective-permute-start(bf16[768,512]{1,0:T(8,128)(2,1)} %get-tuple-element.76), channel_id=1, source_target_pairs={{8,0},{16,8},{24,16},{9,1},{17,9},{25,17},{10,2},{18,10},{26,18},{... | collective-permute-start | bytes 2359304 | tf_op jit(solution)/shard_map/ppermute | solution.py:939
  90.7 30.5 %collective-permute-start.8 = (bf16[176,1024]{1,0:T(8,128)(2,1)}, bf16[176,1024]{1,0:T(8,128)(2,1)S(1)}, u32[]{:S(2)}, u32[]{:S(2)}) collective-permute-start(bf16[176,1024]{1,0:T(8,128)(2,1)} %get-tuple-element.77), channel_id=1, source_target_pairs={{0,1},{1,2},{2,3},{3,4},{4,5},{5,6},{6,7},{8,9},{9,10},{10,11},{11... | collective-permute-start | bytes 1081352 | tf_op jit(solution)/shard_map/ppermute | solution.py:939
  95.1 27.4 %collective-permute-start.9 = (bf16[176,1024]{1,0:T(8,128)(2,1)}, bf16[176,1024]{1,0:T(8,128)(2,1)S(1)}, u32[]{:S(2)}, u32[]{:S(2)}) collective-permute-start(bf16[176,1024]{1,0:T(8,128)(2,1)} %get-tuple-element.78), channel_id=1, source_target_pairs={{1,0},{2,1},{3,2},{4,3},{5,4},{6,5},{7,6},{9,8},{10,9},{11,10},{12... | collective-permute-start | bytes 1081352 | tf_op jit(solution)/shard_map/ppermute | solution.py:939
  96.4 7.6 %collective-permute-start.10 = (bf16[80,256]{1,0:T(8,128)(2,1)}, bf16[80,256]{1,0:T(8,128)(2,1)S(1)}, u32[]{:S(2)}, u32[]{:S(2)}) collective-permute-start(bf16[80,256]{1,0:T(8,128)(2,1)} %get-tuple-element.80), channel_id=1, source_target_pairs={{0,16},{8,24},{16,0},{24,8},{1,17},{9,25},{17,1},{25,9},{2,18},{10... | collective-permute-start | bytes 122888 | tf_op jit(solution)/shard_map/ppermute | solution.py:946
  103.9 0.6 copy-start.12
  103.9 0.9 copy-start.2
  103.9 1.1 copy-start.3
  107.8 20.5 %collective-permute-start.11 = (bf16[448,256]{1,0:T(8,128)(2,1)}, bf16[448,256]{1,0:T(8,128)(2,1)S(1)}, u32[]{:S(2)}, u32[]{:S(2)}) collective-permute-start(bf16[448,256]{1,0:T(8,128)(2,1)} %get-tuple-element.82), channel_id=1, source_target_pairs={{0,1},{1,2},{2,3},{3,4},{4,5},{5,6},{6,7},{8,9},{9,10},{10,11},{11... | collective-permute-start | bytes 688136 | tf_op jit(solution)/shard_map/ppermute | solution.py:939
  112.2 16.1 %collective-permute-start.12 = (bf16[448,256]{1,0:T(8,128)(2,1)}, bf16[448,256]{1,0:T(8,128)(2,1)S(1)}, u32[]{:S(2)}, u32[]{:S(2)}) collective-permute-start(bf16[448,256]{1,0:T(8,128)(2,1)} %get-tuple-element.83), channel_id=1, source_target_pairs={{1,0},{2,1},{3,2},{4,3},{5,4},{6,5},{7,6},{9,8},{10,9},{11,10},{12... | collective-permute-start | bytes 688136 | tf_op jit(solution)/shard_map/ppermute | solution.py:939
  113.5 10.5 %collective-permute-start.13 = (bf16[256,256]{1,0:T(8,128)(2,1)}, bf16[256,256]{1,0:T(8,128)(2,1)S(1)}, u32[]{:S(2)}, u32[]{:S(2)}) collective-permute-start(bf16[256,256]{1,0:T(8,128)(2,1)} %get-tuple-element.84), channel_id=1, source_target_pairs={{0,2},{1,3},{2,4},{3,5},{4,6},{5,7},{8,10},{9,11},{10,12},{11,13},... | collective-permute-start | bytes 393224 | tf_op jit(solution)/shard_map/ppermute | solution.py:939
  121.2 7.1 %copy-start.6 = (bf16[176,1024]{1,0:T(8,128)(2,1)}, bf16[176,1024]{1,0:T(8,128)(2,1)S(1)}, u32[]{:S(2)}) copy-start(bf16[176,1024]{1,0:T(8,128)(2,1)S(1)} %collective-permute-done.8.refs_7_) | copy-start | bytes 1081348
  121.2 7.1 %collective-permute-start.14 = (bf16[256,256]{1,0:T(8,128)(2,1)}, bf16[256,256]{1,0:T(8,128)(2,1)S(1)}, u32[]{:S(2)}, u32[]{:S(2)}) collective-permute-start(bf16[256,256]{1,0:T(8,128)(2,1)} %get-tuple-element.85), channel_id=1, source_target_pairs={{2,0},{3,1},{4,2},{5,3},{6,4},{7,5},{10,8},{11,9},{12,10},{13,11},... | collective-permute-start | bytes 393224 | tf_op jit(solution)/shard_map/ppermute | solution.py:939
  122.5 5.8 %copy-start.7 = (bf16[176,1024]{1,0:T(8,128)(2,1)}, bf16[176,1024]{1,0:T(8,128)(2,1)S(1)}, u32[]{:S(2)}) copy-start(bf16[176,1024]{1,0:T(8,128)(2,1)S(1)} %collective-permute-done.9.refs_8_) | copy-start | bytes 1081348
  124.0 4.3 %copy-start.13 = (bf16[256,256]{1,0:T(8,128)(2,1)}, bf16[256,256]{1,0:T(8,128)(2,1)S(1)}, u32[]{:S(2)}) copy-start(bf16[256,256]{1,0:T(8,128)(2,1)S(1)} %collective-permute-done.13.refs_12_) | copy-start | bytes 393220
  128.3 0.7 copy-start.14
  128.3 0.8 copy-start.8
  128.3 0.8 copy-start.9
